TPU v7x, 512 devices: a whole 4x4x16 slice. The times are simulated.
512 devices in a mesh: train: 32 (over z_lo, y, core), col: 16 (over x, z_hi).
Axes of the slice: x: 4, y: 4, z: 16 (z_hi: 4, z_lo: 4; z = z_hi * 4 + z_lo), core: 2. Of those that a mesh axis runs over, the one named last changes fastest.
Arguments:
- train_grads: bfloat16 [32768, 32768], P('train', 'col'), may hold values from -0.03125 to 0.03125
- test_grads: bfloat16 [1024, 32768], P('train', 'col'), may hold values from -6 to 6
- precond: bfloat16 [256, 128, 128], P('col'), may hold values from -2 to 4
Outputs:
- scores: bfloat16 [1024, 32768], P('col', 'train')
All inputs are finite; a program needn't handle non-finite values.
Results may differ from a plain program's by a relative error of at most 0.0049.
Values may be sent and summed in bfloat16 or wider, within the bound.
No kernel may reach another device: no remote copies, remote signals or barrier semaphores. Data moves between devices by JAX's collectives and lax.ppermute only.
A program may use at most 64 MiB of HBM per device.

v0:
```python
import jax
import jax.numpy as jnp
from jax import lax
from jax.sharding import PartitionSpec as P


def apply_blocks(rows, precond):
    count = rows.shape[0]
    blocks = precond.shape[0]
    width = precond.shape[1]
    shaped = rows.reshape(count, blocks, width)
    product = jnp.einsum("rbi,bij->rbj", shaped, precond, preferred_element_type=jnp.float32)
    return product.reshape(count, blocks * width).astype(jnp.bfloat16)


def score_rows(source, train_grads):
    return lax.dot_general(
        source, train_grads, (((1,), (1,)), ((), ())), preferred_element_type=jnp.float32
    )


def per_device(train_grads, test_grads, precond):
    conditioned = apply_blocks(lax.all_gather(test_grads, "train", axis=0, tiled=True), precond)
    summed = lax.psum_scatter(
        score_rows(conditioned, train_grads), "col", scatter_dimension=0, tiled=True
    )
    return summed.astype(jnp.bfloat16)


def solution(mesh):
    in_specs = (P("train", "col"), P("train", "col"), P("col", None, None))
    out_specs = P("col", "train")
    return jax.shard_map(
        per_device, mesh=mesh, in_specs=in_specs, out_specs=out_specs, check_vma=False
    )
```

profile of v0, /device:TPU:1, one launch (start us, length us, event | category | flops | bytes accessed | tf_op | source)
XLA Modules:
  0.0 263.3 jit_solution(18368376425690222354)
XLA Ops:
  6.5 0.0 copy-start
  6.5 0.0 all-gather.2.cloned.1.call-start
  6.5 0.7 all-gather.2.cloned.1.call-update
  7.3 0.0 reduce-scatter.2.cloned.1.call-start
  7.3 76.0 %all-gather.2.cloned.1.call-done = bf16[1024,2048]{1,0:T(8,128)(2,1)} async-done(((bf16[32,2048]{1,0:T(8,128)(2,1)}), bf16[1024,2048]{1,0:T(8,128)(2,1)}) %all-gather.2.cloned.1.call-update) | async-done | bytes 4194320 | tf_op jit(solution)/shard_map/all_gather | solution.py:23
  83.3 6.4 %copy.8 = bf16[1024,2048]{0,1:T(8,128)(2,1)} copy(bf16[1024,2048]{1,0:T(8,128)(2,1)} %all-gather.2.cloned.1.call-done) | data formatting | bytes 8388608 | tf_op jit(solution)/shard_map/all_gather | solution.py:23
  89.7 0.0 copy-done
  89.8 0.0 copy-start.1
  89.8 3.6 %convolution_convert_fusion = bf16[16,128,1024]{2,1,0:T(8,128)(2,1)S(1)} fusion(bf16[16,128,128]{2,1,0:T(8,128)(2,1)S(1)} %copy-done, bf16[1024,16,128]{0,2,1:T(8,128)(2,1)} %bitcast.8), kind=kOutput, calls=%fused_computation | convolution fusion | flops 538968064 | bytes 8912896 | tf_op jit(solution)/shard_map/rbi,bij->rbj/dot_general | solution.py:12
  93.4 0.0 copy-done.1
  93.4 6.1 %fusion = f32[1024,1024]{1,0:T(8,128)} fusion(bf16[1024,2048]{0,1:T(8,128)(2,1)S(1)} %bitcast.9, bf16[1024,2048]{1,0:T(8,128)(2,1)S(1)} %copy-done.1), kind=kOutput, calls=%fused_computation.1 | convolution fusion | flops 4294967296 | bytes 12582912 | tf_op jit(solution)/shard_map/dot_general | solution.py:17
  99.5 0.0 reduce-scatter.2.cloned.1.call-update
  99.5 155.3 %reduce-scatter.2.cloned.1.call-done = f32[64,1024]{1,0:T(8,128)} async-done(((f32[1024,1024]{1,0:T(8,128)}), f32[64,1024]{1,0:T(8,128)}) %reduce-scatter.2.cloned.1.call-update) | async-done | bytes 262160 | tf_op jit(solution)/shard_map/reduce_scatter | solution.py:24
  254.9 1.6 convert_element_type.15
Async XLA Ops:
  6.5 83.2 %copy-start = (bf16[16,128,128]{2,1,0:T(8,128)(2,1)S(1)}, bf16[16,128,128]{2,1,0:T(8,128)(2,1)}, u32[]{:S(2)}) copy-start(bf16[16,128,128]{2,1,0:T(8,128)(2,1)} %param.5) | copy-start | bytes 1572868
  6.5 76.8 %all-gather.2.cloned.1.call-start = ((), (), s32[]{:S(2)}) async-start(), calls=%async_computation.1 | async-start | bytes 4325376 | tf_op jit(solution)/shard_map/all_gather | solution.py:23
  7.3 247.6 %reduce-scatter.2.cloned.1.call-start = ((), (), s32[]{:S(2)}) async-start(), calls=%async_computation.2 | async-start | bytes 4456448 | tf_op jit(solution)/shard_map/reduce_scatter | solution.py:24
  89.8 3.6 %copy-start.1 = (bf16[1024,2048]{1,0:T(8,128)(2,1)S(1)}, bf16[1024,2048]{1,0:T(8,128)(2,1)}, u32[]{:S(2)}) copy-start(bf16[1024,2048]{1,0:T(8,128)(2,1)} %param.3) | copy-start | bytes 12582916
Sparse Core Ops, SparseCore 0:
  9.5 73.7 all-gather.1
  99.7 155.1 reduce-scatter.1
where the time goes:
time: 264 us; the launch traced here: 263 us
  waiting for transfers between devices  232 us (88%)
  between operations  13.4 us (5%)
  matrix products  9.75 us (4%)
  local copies, waits for them, and re-layouts  6.45 us (2%)
    reduce_scatter x1, waiting for transfers between devices, per_device(): lax.psum_scatter(score_rows(conditioned, train_grads), 'col', scatter_dim...  155 us
    all_gather x1, waiting for transfers between devices, per_device(): lax.all_gather(test_grads, 'train', axis=0, tiled=True)  76 us
    all_gather x1, local copies, waits for them, and re-layouts, per_device(): lax.all_gather(test_grads, 'train', axis=0, tiled=True)  6.45 us
    dot_general x1, matrix products, score_rows(): lax.dot_general(source, train_grads, (((1,), (1,)), ((), ())), preferred_...  6.12 us
  transfers between devices with their start and end apart: 2, of which 2 were waited for; matrix products, arithmetic and copies ran while one was open for 0% of the time, Pallas kernels for 0%

commit v1 on v0

v1 whole, which is shorter than its diff:
```python
import jax
import jax.numpy as jnp
import numpy as np
from jax import lax
from jax.experimental import pallas as pl
from jax.experimental.pallas import tpu as pltpu
from jax.sharding import Mesh, PartitionSpec as P

AXES = ("zl", "y", "core", "x", "zh")
SIZES = (4, 4, 2, 4, 4)
BLOCK = 128


def condition_kernel(rows_ref, precond_ref, out_ref):
    for b in range(precond_ref.shape[0]):
        cols = pl.ds(b * BLOCK, BLOCK)
        out_ref[:, cols] = jnp.dot(
            rows_ref[:, cols], precond_ref[b], preferred_element_type=jnp.float32
        ).astype(out_ref.dtype)


def condition(rows, precond):
    return pl.pallas_call(
        condition_kernel,
        out_shape=jax.ShapeDtypeStruct(rows.shape, rows.dtype),
        in_specs=[pl.BlockSpec(memory_space=pltpu.VMEM)] * 2,
        out_specs=pl.BlockSpec(memory_space=pltpu.VMEM),
    )(rows, precond)


def shift(array, axis, step):
    size = SIZES[AXES.index(axis)]
    return lax.ppermute(array, axis, [(i, (i + step) % size) for i in range(size)])


def dot_t(rows, train):
    out = lax.dot_general(
        rows, train, (((1,), (1,)), ((), ())), preferred_element_type=jnp.float32
    )
    return out.astype(jnp.bfloat16)


def f32_sum(arrays):
    total = arrays[0].astype(jnp.float32)
    for a in arrays[1:]:
        total = total + a.astype(jnp.float32)
    return total


def per_device(train_grads, test_grads, precond):
    zl, y, core = lax.axis_index("zl"), lax.axis_index("y"), lax.axis_index("core")
    x, zh = lax.axis_index("x"), lax.axis_index("zh")
    count = test_grads.shape[0]
    width = train_grads.shape[0]

    own = condition(test_grads, precond)
    line = jnp.concatenate([own] + [shift(own, "zl", k) for k in (1, 2, 3)], axis=0)
    plane = jnp.concatenate([line] + [shift(line, "y", m) for m in (1, 2, 3)], axis=0)
    other = shift(plane, "core", 1)

    shape = (4, 4, count, width)
    part = [dot_t(plane, train_grads).reshape(shape), dot_t(other, train_grads).reshape(shape)]

    def for_x(step):
        k = jnp.mod(zl - x - step, 4)
        return jnp.stack(
            [lax.dynamic_index_in_dim(p, k, axis=1, keepdims=False) for p in part], axis=1
        )

    got = [for_x(0)] + [shift(for_x(j), "x", j) for j in (1, 2, 3)]
    total = f32_sum(got)

    def for_zh(step):
        m = jnp.mod(y - zh - step, 4)
        return lax.dynamic_index_in_dim(total, m, axis=0, keepdims=False)

    last = [for_zh(0)] + [shift(for_zh(i).astype(jnp.bfloat16), "zh", i) for i in (1, 2, 3)]
    scores = f32_sum(last).astype(jnp.bfloat16)
    scores = jnp.where(core == 0, scores, scores[::-1])
    return scores.reshape(2 * count, width)


def solution(mesh):
    fine = Mesh(mesh.devices.reshape(SIZES), AXES)
    train, col = ("zl", "y", "core"), ("x", "zh")
    return jax.shard_map(
        per_device,
        mesh=fine,
        in_specs=(P(train, col), P(train, col), P(col, None, None)),
        out_specs=P(col, train),
        check_vma=False,
    )
```

time: 264 us -> 138 us (0.52)
  the two profiles are of different devices: /device:TPU:1 before, /device:TPU:105 now
where the time goes in v1:
time: 138 us
  waiting for transfers between devices  69 us (50%)
  starting transfers between devices  52.9 us (38%)
  matrix products  8.66 us (6%)
  other arithmetic  3.22 us (2%)
  Pallas kernels  2.02 us (1%)
    ppermute x13, waiting for transfers between devices, shift(): lax.ppermute(array, axis, [(i, (i + step) % size) for i in range(size)])  69 us
    ppermute x13, starting transfers between devices, shift(): lax.ppermute(array, axis, [(i, (i + step) % size) for i in range(size)])  52.9 us
    dot_general x2, matrix products, dot_t(): lax.dot_general(rows, train, (((1,), (1,)), ((), ())), preferred_element_...  8.66 us
  transfers between devices with their start and end apart: 13, of which 8 were waited for; matrix products, arithmetic and copies ran while one was open for 4% of the time, Pallas kernels for 0%

profile of v1, /device:TPU:105, one launch (start us, length us, event | category | flops | bytes accessed | tf_op | source)
XLA Modules:
  0.0 137.6 jit_solution(3814538532619320892)
XLA Ops:
  0.0 2.0 %shard_map.37 = bf16[32,2048]{1,0:T(8,128)(2,1)} custom-call(bf16[32,2048]{1,0:T(8,128)(2,1)} %rows_ref.1, bf16[16,128,128]{2,1,0:T(8,128)(2,1)} %precond_ref.1), custom_call_target="tpu_custom_call" | custom-call | tf_op jit(solution)/shard_map/pallas_call | solution.py:23
  2.0 1.9 %collective-permute-start = (bf16[32,2048]{1,0:T(8,128)(2,1)}, bf16[32,2048]{1,0:T(8,128)(2,1)S(1)}, u32[]{:S(2)}, u32[]{:S(2)}) collective-permute-start(bf16[32,2048]{1,0:T(8,128)(2,1)} %shard_map.37), channel_id=1, source_target_pairs={{0,128},{128,256},{256,384},{384,0},{1,129},{129,257},{257,385},{3... | collective-permute-start | bytes 393224 | tf_op jit(solution)/shard_map/ppermute | solution.py:33
  3.9 2.9 %collective-permute-start.1 = (bf16[32,2048]{1,0:T(8,128)(2,1)}, bf16[32,2048]{1,0:T(8,128)(2,1)S(1)}, u32[]{:S(2)}, u32[]{:S(2)}) collective-permute-start(bf16[32,2048]{1,0:T(8,128)(2,1)} %shard_map.37), channel_id=1, source_target_pairs={{0,256},{128,384},{256,0},{384,128},{1,257},{129,385},{257,1},{385... | collective-permute-start | bytes 393224 | tf_op jit(solution)/shard_map/ppermute | solution.py:33
  6.9 2.4 %collective-permute-start.2 = (bf16[32,2048]{1,0:T(8,128)(2,1)}, bf16[32,2048]{1,0:T(8,128)(2,1)S(1)}, u32[]{:S(2)}, u32[]{:S(2)}) collective-permute-start(bf16[32,2048]{1,0:T(8,128)(2,1)} %shard_map.37), channel_id=1, source_target_pairs={{0,384},{128,0},{256,128},{384,256},{1,385},{129,1},{257,129},{385... | collective-permute-start | bytes 393224 | tf_op jit(solution)/shard_map/ppermute | solution.py:33
  9.2 0.9 constant_dynamic-update-slice_fusion.6
  10.2 0.0 collective-permute-done
  10.2 6.8 %collective-permute-done.1 = bf16[32,2048]{1,0:T(8,128)(2,1)S(1)} collective-permute-done((bf16[32,2048]{1,0:T(8,128)(2,1)}, bf16[32,2048]{1,0:T(8,128)(2,1)S(1)}, u32[]{:S(2)}, u32[]{:S(2)}) %collective-permute-start.1) | collective-permute-done | bytes 131104 | tf_op jit(solution)/shard_map/ppermute | solution.py:33
  16.9 0.0 collective-permute-done.2
  16.9 0.9 pad_maximum_fusion
  17.9 3.2 %collective-permute-start.3 = (bf16[128,2048]{1,0:T(8,128)(2,1)S(1)}, bf16[128,2048]{1,0:T(8,128)(2,1)S(1)}, u32[]{:S(2)}, u32[]{:S(2)}) collective-permute-start(bf16[128,2048]{1,0:T(8,128)(2,1)S(1)} %pad_maximum_fusion), channel_id=1, source_target_pairs={{0,32},{32,64},{64,96},{96,0},{1,33},{33,65},{65,97},{97,1},{2,34}... | collective-permute-start | bytes 1572872 | tf_op jit(solution)/shard_map/ppermute | solution.py:33
  21.1 2.6 %collective-permute-start.4 = (bf16[128,2048]{1,0:T(8,128)(2,1)S(1)}, bf16[128,2048]{1,0:T(8,128)(2,1)S(1)}, u32[]{:S(2)}, u32[]{:S(2)}) collective-permute-start(bf16[128,2048]{1,0:T(8,128)(2,1)S(1)} %pad_maximum_fusion), channel_id=1, source_target_pairs={{0,64},{32,96},{64,0},{96,32},{1,65},{33,97},{65,1},{97,33},{2,66}... | collective-permute-start | bytes 1572872 | tf_op jit(solution)/shard_map/ppermute | solution.py:33
  23.7 4.0 %collective-permute-start.5 = (bf16[128,2048]{1,0:T(8,128)(2,1)S(1)}, bf16[128,2048]{1,0:T(8,128)(2,1)S(1)}, u32[]{:S(2)}, u32[]{:S(2)}) collective-permute-start(bf16[128,2048]{1,0:T(8,128)(2,1)S(1)} %pad_maximum_fusion), channel_id=1, source_target_pairs={{0,96},{32,0},{64,32},{96,64},{1,97},{33,1},{65,33},{97,65},{2,98}... | collective-permute-start | bytes 1572872 | tf_op jit(solution)/shard_map/ppermute | solution.py:33
  27.8 3.9 %collective-permute-done.3 = bf16[128,2048]{1,0:T(8,128)(2,1)S(1)} collective-permute-done((bf16[128,2048]{1,0:T(8,128)(2,1)S(1)}, bf16[128,2048]{1,0:T(8,128)(2,1)S(1)}, u32[]{:S(2)}, u32[]{:S(2)}) %collective-permute-start.3) | collective-permute-done | bytes 524320 | tf_op jit(solution)/shard_map/ppermute | solution.py:33
  31.7 4.4 %collective-permute-done.4 = bf16[128,2048]{1,0:T(8,128)(2,1)S(1)} collective-permute-done((bf16[128,2048]{1,0:T(8,128)(2,1)S(1)}, bf16[128,2048]{1,0:T(8,128)(2,1)S(1)}, u32[]{:S(2)}, u32[]{:S(2)}) %collective-permute-start.4) | collective-permute-done | bytes 524320 | tf_op jit(solution)/shard_map/ppermute | solution.py:33
  36.2 13.4 %collective-permute-done.5 = bf16[128,2048]{1,0:T(8,128)(2,1)S(1)} collective-permute-done((bf16[128,2048]{1,0:T(8,128)(2,1)S(1)}, bf16[128,2048]{1,0:T(8,128)(2,1)S(1)}, u32[]{:S(2)}, u32[]{:S(2)}) %collective-permute-start.5) | collective-permute-done | bytes 524320 | tf_op jit(solution)/shard_map/ppermute | solution.py:33
  49.6 2.4 %collective-permute-start.6 = (bf16[512,2048]{1,0:T(8,128)(2,1)S(1)}, bf16[512,2048]{1,0:T(8,128)(2,1)}, u32[]{:S(2)}, u32[]{:S(2)}) collective-permute-start(bf16[512,2048]{1,0:T(8,128)(2,1)S(1)} %constant_dynamic-update-slice_fusion), channel_id=1, source_target_pairs={{0,16},{16,0},{1,17},{17,1},{2,18},{18,2},{3,19},{19,3},{4,20},{20... | collective-permute-start | bytes 6291464 | tf_op jit(solution)/shard_map/ppermute | solution.py:33
  52.1 0.0 copy-start
  52.1 4.7 %convolution_convert_fusion.1 = bf16[512,1024]{1,0:T(8,128)(2,1)S(1)} fusion(bf16[512,2048]{1,0:T(8,128)(2,1)S(1)} %constant_dynamic-update-slice_fusion, bf16[1024,2048]{1,0:T(8,128)(2,1)} %param.3), kind=kOutput, calls=%fused_computation.1 | convolution fusion | flops 2148007936 | bytes 7340032 | tf_op jit(solution)/shard_map/dot_general | solution.py:37
  56.8 0.0 collective-permute-done.6
  56.8 0.0 copy-done
  56.9 4.0 %convolution_convert_fusion = bf16[512,1024]{1,0:T(8,128)(2,1)S(1)} fusion(bf16[512,2048]{1,0:T(8,128)(2,1)} %collective-permute-done.6, bf16[1024,2048]{1,0:T(8,128)(2,1)S(1)} %copy-done), kind=kOutput, calls=%fused_computation | convolution fusion | flops 2148007936 | bytes 7340032 | tf_op jit(solution)/shard_map/dot_general | solution.py:37
  60.8 0.2 constant_dynamic-slice_fusion.6
  61.0 0.1 pad_maximum_fusion.3
  61.1 4.4 %collective-permute-start.9 = (bf16[4,2,32,1024]{3,2,1,0:T(8,128)(2,1)S(1)}, bf16[4,2,32,1024]{3,2,1,0:T(8,128)(2,1)S(1)}, u32[]{:S(2)}, u32[]{:S(2)}) collective-permute-start(bf16[4,2,32,1024]{3,2,1,0:T(8,128)(2,1)S(1)} %pad_maximum_fusion.3), channel_id=1, source_target_pairs={{0,12},{4,0},{8,4},{12,8},{1,13},{5,1},{9,5},{13,9},{2,14},{6,2},{... | collective-permute-start | bytes 1572872 | tf_op jit(solution)/shard_map/ppermute | solution.py:33
  65.5 0.1 pad_maximum_fusion.2
  65.5 2.4 %collective-permute-start.8 = (bf16[4,2,32,1024]{3,2,1,0:T(8,128)(2,1)S(1)}, bf16[4,2,32,1024]{3,2,1,0:T(8,128)(2,1)S(1)}, u32[]{:S(2)}, u32[]{:S(2)}) collective-permute-start(bf16[4,2,32,1024]{3,2,1,0:T(8,128)(2,1)S(1)} %pad_maximum_fusion.2), channel_id=1, source_target_pairs={{0,8},{4,12},{8,0},{12,4},{1,9},{5,13},{9,1},{13,5},{2,10},{6,14},... | collective-permute-start | bytes 1572872 | tf_op jit(solution)/shard_map/ppermute | solution.py:33
  68.0 0.1 pad_maximum_fusion.1
  68.0 2.5 %collective-permute-start.7 = (bf16[4,2,32,1024]{3,2,1,0:T(8,128)(2,1)S(1)}, bf16[4,2,32,1024]{3,2,1,0:T(8,128)(2,1)}, u32[]{:S(2)}, u32[]{:S(2)}) collective-permute-start(bf16[4,2,32,1024]{3,2,1,0:T(8,128)(2,1)S(1)} %pad_maximum_fusion.1), channel_id=1, source_target_pairs={{0,4},{4,8},{8,12},{12,0},{1,5},{5,9},{9,13},{13,1},{2,6},{6,10},{... | collective-permute-start | bytes 1572872 | tf_op jit(solution)/shard_map/ppermute | solution.py:33
  70.6 17.3 %collective-permute-done.9 = bf16[4,2,32,1024]{3,2,1,0:T(8,128)(2,1)S(1)} collective-permute-done((bf16[4,2,32,1024]{3,2,1,0:T(8,128)(2,1)S(1)}, bf16[4,2,32,1024]{3,2,1,0:T(8,128)(2,1)S(1)}, u32[]{:S(2)}, u32[]{:S(2)}) %collective-permute-start.9) | collective-permute-done | bytes 524320 | tf_op jit(solution)/shard_map/ppermute | solution.py:33
  87.9 0.0 collective-permute-done.8
  87.9 6.2 %collective-permute-done.7 = bf16[4,2,32,1024]{3,2,1,0:T(8,128)(2,1)} collective-permute-done((bf16[4,2,32,1024]{3,2,1,0:T(8,128)(2,1)S(1)}, bf16[4,2,32,1024]{3,2,1,0:T(8,128)(2,1)}, u32[]{:S(2)}, u32[]{:S(2)}) %collective-permute-start.7) | collective-permute-done | bytes 524320 | tf_op jit(solution)/shard_map/ppermute | solution.py:33
  94.1 1.4 convert_add_fusion
  95.5 0.1 fusion.3
  95.6 12.0 %collective-permute-start.12 = (bf16[2,32,1024]{2,1,0:T(8,128)(2,1)S(1)}, bf16[2,32,1024]{2,1,0:T(8,128)(2,1)S(1)}, u32[]{:S(2)}, u32[]{:S(2)}) collective-permute-start(bf16[2,32,1024]{2,1,0:T(8,128)(2,1)S(1)} %get-tuple-element.6), channel_id=1, source_target_pairs={{0,3},{1,0},{2,1},{3,2},{4,7},{5,4},{6,5},{7,6},{8,11},{9,8},{10,9... | collective-permute-start | bytes 393224 | tf_op jit(solution)/shard_map/ppermute | solution.py:33
  107.6 4.9 %collective-permute-start.11 = (bf16[2,32,1024]{2,1,0:T(8,128)(2,1)S(1)}, bf16[2,32,1024]{2,1,0:T(8,128)(2,1)S(1)}, u32[]{:S(2)}, u32[]{:S(2)}) collective-permute-start(bf16[2,32,1024]{2,1,0:T(8,128)(2,1)S(1)} %get-tuple-element.7), channel_id=1, source_target_pairs={{0,2},{1,3},{2,0},{3,1},{4,6},{5,7},{6,4},{7,5},{8,10},{9,11},{10,... | collective-permute-start | bytes 393224 | tf_op jit(solution)/shard_map/ppermute | solution.py:33
  112.5 7.3 %collective-permute-start.10 = (bf16[2,32,1024]{2,1,0:T(8,128)(2,1)S(1)}, bf16[2,32,1024]{2,1,0:T(8,128)(2,1)S(1)}, u32[]{:S(2)}, u32[]{:S(2)}) collective-permute-start(bf16[2,32,1024]{2,1,0:T(8,128)(2,1)S(1)} %get-tuple-element.5), channel_id=1, source_target_pairs={{0,1},{1,2},{2,3},{3,0},{4,5},{5,6},{6,7},{7,4},{8,9},{9,10},{10,1... | collective-permute-start | bytes 393224 | tf_op jit(solution)/shard_map/ppermute | solution.py:33
  119.8 0.0 collective-permute-done.12
  119.8 6.4 %collective-permute-done.11 = bf16[2,32,1024]{2,1,0:T(8,128)(2,1)S(1)} collective-permute-done((bf16[2,32,1024]{2,1,0:T(8,128)(2,1)S(1)}, bf16[2,32,1024]{2,1,0:T(8,128)(2,1)S(1)}, u32[]{:S(2)}, u32[]{:S(2)}) %collective-permute-start.11) | collective-permute-done | bytes 131104 | tf_op jit(solution)/shard_map/ppermute | solution.py:33
  126.2 10.6 %collective-permute-done.10 = bf16[2,32,1024]{2,1,0:T(8,128)(2,1)S(1)} collective-permute-done((bf16[2,32,1024]{2,1,0:T(8,128)(2,1)S(1)}, bf16[2,32,1024]{2,1,0:T(8,128)(2,1)S(1)}, u32[]{:S(2)}, u32[]{:S(2)}) %collective-permute-start.10) | collective-permute-done | bytes 131104 | tf_op jit(solution)/shard_map/ppermute | solution.py:33
  136.8 0.1 fusion.2
  136.9 0.7 reverse_select_fusion
  (6 shorter events, 0.1 us)
Async XLA Ops:
  2.0 8.1 %collective-permute-start = (bf16[32,2048]{1,0:T(8,128)(2,1)}, bf16[32,2048]{1,0:T(8,128)(2,1)S(1)}, u32[]{:S(2)}, u32[]{:S(2)}) collective-permute-start(bf16[32,2048]{1,0:T(8,128)(2,1)} %shard_map.37), channel_id=1, source_target_pairs={{0,128},{128,256},{256,384},{384,0},{1,129},{129,257},{257,385},{3... | collective-permute-start | bytes 393224 | tf_op jit(solution)/shard_map/ppermute | solution.py:33
  3.9 13.0 %collective-permute-start.1 = (bf16[32,2048]{1,0:T(8,128)(2,1)}, bf16[32,2048]{1,0:T(8,128)(2,1)S(1)}, u32[]{:S(2)}, u32[]{:S(2)}) collective-permute-start(bf16[32,2048]{1,0:T(8,128)(2,1)} %shard_map.37), channel_id=1, source_target_pairs={{0,256},{128,384},{256,0},{384,128},{1,257},{129,385},{257,1},{385... | collective-permute-start | bytes 393224 | tf_op jit(solution)/shard_map/ppermute | solution.py:33
  6.9 10.1 %collective-permute-start.2 = (bf16[32,2048]{1,0:T(8,128)(2,1)}, bf16[32,2048]{1,0:T(8,128)(2,1)S(1)}, u32[]{:S(2)}, u32[]{:S(2)}) collective-permute-start(bf16[32,2048]{1,0:T(8,128)(2,1)} %shard_map.37), channel_id=1, source_target_pairs={{0,384},{128,0},{256,128},{384,256},{1,385},{129,1},{257,129},{385... | collective-permute-start | bytes 393224 | tf_op jit(solution)/shard_map/ppermute | solution.py:33
  17.9 13.8 %collective-permute-start.3 = (bf16[128,2048]{1,0:T(8,128)(2,1)S(1)}, bf16[128,2048]{1,0:T(8,128)(2,1)S(1)}, u32[]{:S(2)}, u32[]{:S(2)}) collective-permute-start(bf16[128,2048]{1,0:T(8,128)(2,1)S(1)} %pad_maximum_fusion), channel_id=1, source_target_pairs={{0,32},{32,64},{64,96},{96,0},{1,33},{33,65},{65,97},{97,1},{2,34}... | collective-permute-start | bytes 1572872 | tf_op jit(solution)/shard_map/ppermute | solution.py:33
  21.1 15.0 %collective-permute-start.4 = (bf16[128,2048]{1,0:T(8,128)(2,1)S(1)}, bf16[128,2048]{1,0:T(8,128)(2,1)S(1)}, u32[]{:S(2)}, u32[]{:S(2)}) collective-permute-start(bf16[128,2048]{1,0:T(8,128)(2,1)S(1)} %pad_maximum_fusion), channel_id=1, source_target_pairs={{0,64},{32,96},{64,0},{96,32},{1,65},{33,97},{65,1},{97,33},{2,66}... | collective-permute-start | bytes 1572872 | tf_op jit(solution)/shard_map/ppermute | solution.py:33
  23.7 25.8 %collective-permute-start.5 = (bf16[128,2048]{1,0:T(8,128)(2,1)S(1)}, bf16[128,2048]{1,0:T(8,128)(2,1)S(1)}, u32[]{:S(2)}, u32[]{:S(2)}) collective-permute-start(bf16[128,2048]{1,0:T(8,128)(2,1)S(1)} %pad_maximum_fusion), channel_id=1, source_target_pairs={{0,96},{32,0},{64,32},{96,64},{1,97},{33,1},{65,33},{97,65},{2,98}... | collective-permute-start | bytes 1572872 | tf_op jit(solution)/shard_map/ppermute | solution.py:33
  49.6 7.2 %collective-permute-start.6 = (bf16[512,2048]{1,0:T(8,128)(2,1)S(1)}, bf16[512,2048]{1,0:T(8,128)(2,1)}, u32[]{:S(2)}, u32[]{:S(2)}) collective-permute-start(bf16[512,2048]{1,0:T(8,128)(2,1)S(1)} %constant_dynamic-update-slice_fusion), channel_id=1, source_target_pairs={{0,16},{16,0},{1,17},{17,1},{2,18},{18,2},{3,19},{19,3},{4,20},{20... | collective-permute-start | bytes 6291464 | tf_op jit(solution)/shard_map/ppermute | solution.py:33
  52.1 4.7 %copy-start = (bf16[1024,2048]{1,0:T(8,128)(2,1)S(1)}, bf16[1024,2048]{1,0:T(8,128)(2,1)}, u32[]{:S(2)}) copy-start(bf16[1024,2048]{1,0:T(8,128)(2,1)} %param.3) | copy-start | bytes 12582916
  61.1 26.8 %collective-permute-start.9 = (bf16[4,2,32,1024]{3,2,1,0:T(8,128)(2,1)S(1)}, bf16[4,2,32,1024]{3,2,1,0:T(8,128)(2,1)S(1)}, u32[]{:S(2)}, u32[]{:S(2)}) collective-permute-start(bf16[4,2,32,1024]{3,2,1,0:T(8,128)(2,1)S(1)} %pad_maximum_fusion.3), channel_id=1, source_target_pairs={{0,12},{4,0},{8,4},{12,8},{1,13},{5,1},{9,5},{13,9},{2,14},{6,2},{... | collective-permute-start | bytes 1572872 | tf_op jit(solution)/shard_map/ppermute | solution.py:33
  65.5 22.4 %collective-permute-start.8 = (bf16[4,2,32,1024]{3,2,1,0:T(8,128)(2,1)S(1)}, bf16[4,2,32,1024]{3,2,1,0:T(8,128)(2,1)S(1)}, u32[]{:S(2)}, u32[]{:S(2)}) collective-permute-start(bf16[4,2,32,1024]{3,2,1,0:T(8,128)(2,1)S(1)} %pad_maximum_fusion.2), channel_id=1, source_target_pairs={{0,8},{4,12},{8,0},{12,4},{1,9},{5,13},{9,1},{13,5},{2,10},{6,14},... | collective-permute-start | bytes 1572872 | tf_op jit(solution)/shard_map/ppermute | solution.py:33
  68.0 26.1 %collective-permute-start.7 = (bf16[4,2,32,1024]{3,2,1,0:T(8,128)(2,1)S(1)}, bf16[4,2,32,1024]{3,2,1,0:T(8,128)(2,1)}, u32[]{:S(2)}, u32[]{:S(2)}) collective-permute-start(bf16[4,2,32,1024]{3,2,1,0:T(8,128)(2,1)S(1)} %pad_maximum_fusion.1), channel_id=1, source_target_pairs={{0,4},{4,8},{8,12},{12,0},{1,5},{5,9},{9,13},{13,1},{2,6},{6,10},{... | collective-permute-start | bytes 1572872 | tf_op jit(solution)/shard_map/ppermute | solution.py:33
  95.6 24.2 %collective-permute-start.12 = (bf16[2,32,1024]{2,1,0:T(8,128)(2,1)S(1)}, bf16[2,32,1024]{2,1,0:T(8,128)(2,1)S(1)}, u32[]{:S(2)}, u32[]{:S(2)}) collective-permute-start(bf16[2,32,1024]{2,1,0:T(8,128)(2,1)S(1)} %get-tuple-element.6), channel_id=1, source_target_pairs={{0,3},{1,0},{2,1},{3,2},{4,7},{5,4},{6,5},{7,6},{8,11},{9,8},{10,9... | collective-permute-start | bytes 393224 | tf_op jit(solution)/shard_map/ppermute | solution.py:33
  107.6 18.6 %collective-permute-start.11 = (bf16[2,32,1024]{2,1,0:T(8,128)(2,1)S(1)}, bf16[2,32,1024]{2,1,0:T(8,128)(2,1)S(1)}, u32[]{:S(2)}, u32[]{:S(2)}) collective-permute-start(bf16[2,32,1024]{2,1,0:T(8,128)(2,1)S(1)} %get-tuple-element.7), channel_id=1, source_target_pairs={{0,2},{1,3},{2,0},{3,1},{4,6},{5,7},{6,4},{7,5},{8,10},{9,11},{10,... | collective-permute-start | bytes 393224 | tf_op jit(solution)/shard_map/ppermute | solution.py:33
  112.5 24.3 %collective-permute-start.10 = (bf16[2,32,1024]{2,1,0:T(8,128)(2,1)S(1)}, bf16[2,32,1024]{2,1,0:T(8,128)(2,1)S(1)}, u32[]{:S(2)}, u32[]{:S(2)}) collective-permute-start(bf16[2,32,1024]{2,1,0:T(8,128)(2,1)S(1)} %get-tuple-element.5), channel_id=1, source_target_pairs={{0,1},{1,2},{2,3},{3,0},{4,5},{5,6},{6,7},{7,4},{8,9},{9,10},{10,1... | collective-permute-start | bytes 393224 | tf_op jit(solution)/shard_map/ppermute | solution.py:33

commit v2 on v1

--- a/solution.py
+++ b/solution.py
@@ -1,6 +1,5 @@
 import jax
 import jax.numpy as jnp
-import numpy as np
 from jax import lax
 from jax.experimental import pallas as pl
 from jax.experimental.pallas import tpu as pltpu
@@ -40,11 +39,13 @@
     return out.astype(jnp.bfloat16)
 
 
-def f32_sum(arrays):
-    total = arrays[0].astype(jnp.float32)
-    for a in arrays[1:]:
-        total = total + a.astype(jnp.float32)
-    return total
+def halve_x(array, first):
+    pairs = []
+    for core in range(2):
+        for x in range(4):
+            up = (x + core + (0 if first else 1)) % 2 == 0
+            pairs.append((core * 4 + x, core * 4 + (x + (1 if up else 3)) % 4))
+    return lax.ppermute(array, ("core", "x"), pairs)
 
 
 def per_device(train_grads, test_grads, precond):
@@ -54,28 +55,40 @@
     width = train_grads.shape[0]
 
     own = condition(test_grads, precond)
-    line = jnp.concatenate([own] + [shift(own, "zl", k) for k in (1, 2, 3)], axis=0)
-    plane = jnp.concatenate([line] + [shift(line, "y", m) for m in (1, 2, 3)], axis=0)
+    near = {k: shift(own, "zl", k) for k in (2, 1, 3)}
+    own_y = {m: shift(own, "y", m) for m in (2, 1, 3)}
+    near, own_y = lax.optimization_barrier((near, own_y))
+    rest = jnp.concatenate([near[k] for k in (1, 2, 3)], axis=0)
+    rest_y = {m: shift(rest, "y", m) for m in (2, 1, 3)}
+    plane = [own, rest]
+    for m in (1, 2, 3):
+        plane += [own_y[m], rest_y[m]]
+    plane = jnp.concatenate(plane, axis=0)
     other = shift(plane, "core", 1)
 
     shape = (4, 4, count, width)
     part = [dot_t(plane, train_grads).reshape(shape), dot_t(other, train_grads).reshape(shape)]
 
-    def for_x(step):
-        k = jnp.mod(zl - x - step, 4)
-        return jnp.stack(
-            [lax.dynamic_index_in_dim(p, k, axis=1, keepdims=False) for p in part], axis=1
+    first = jnp.where(jnp.mod(x + core, 2) == 0, 1, 3)
+
+    def block(i, j):
+        m, k = jnp.mod(y - zh - i, 4), jnp.mod(zl - x - j, 4)
+        return jnp.concatenate(
+            [lax.dynamic_slice(p, (m, k, 0, 0), (1, 1, count, width))[0] for p in part], axis=0
         )
 
-    got = [for_x(0)] + [shift(for_x(j), "x", j) for j in (1, 2, 3)]
-    total = f32_sum(got)
+    def sum_x(i):
+        send = jnp.concatenate([block(i, first), block(i, 2)], axis=0)
+        got = halve_x(send, True)
+        keep = block(i, 0).astype(jnp.float32) + got[:2].astype(jnp.float32)
+        back = block(i, 4 - first).astype(jnp.float32) + got[2:].astype(jnp.float32)
+        return keep + halve_x(back.astype(jnp.bfloat16), False).astype(jnp.float32)
 
-    def for_zh(step):
-        m = jnp.mod(y - zh - step, 4)
-        return lax.dynamic_index_in_dim(total, m, axis=0, keepdims=False)
-
-    last = [for_zh(0)] + [shift(for_zh(i).astype(jnp.bfloat16), "zh", i) for i in (1, 2, 3)]
-    scores = f32_sum(last).astype(jnp.bfloat16)
+    sums = {i: sum_x(i) for i in (2, 1, 3, 0)}
+    total = sums[0]
+    for i in (2, 1, 3):
+        total = total + shift(sums[i].astype(jnp.bfloat16), "zh", i).astype(jnp.float32)
+    scores = total.astype(jnp.bfloat16)
     scores = jnp.where(core == 0, scores, scores[::-1])
     return scores.reshape(2 * count, width)
 

time: 138 us -> 126 us (0.913)
  the two profiles are of different devices: /device:TPU:105 before, /device:TPU:1 now
where the time goes in v2:
time: 126 us; the launch traced here: 125 us
  starting transfers between devices  82.5 us (65%)
  waiting for transfers between devices  28.1 us (22%)
  matrix products  8.66 us (7%)
  Pallas kernels  2.02 us (2%)
  local copies, waits for them, and re-layouts  1.53 us (1%)
  other arithmetic  1.27 us (1%)
    ppermute x13, starting transfers between devices, shift(): lax.ppermute(array, axis, [(i, (i + step) % size) for i in range(size)])  59 us
    ppermute x13, waiting for transfers between devices, shift(): lax.ppermute(array, axis, [(i, (i + step) % size) for i in range(size)])  28.1 us
    ppermute x8, starting transfers between devices, halve_x(): return lax.ppermute(array, ('core', 'x'), pairs)  23.6 us
    dot_general x2, matrix products, dot_t(): lax.dot_general(rows, train, (((1,), (1,)), ((), ())), preferred_element_...  8.66 us
  transfers between devices with their start and end apart: 21, of which 7 were waited for; matrix products, arithmetic and copies ran while one was open for 5% of the time, Pallas kernels for 0%

profile of v2, /device:TPU:1, one launch (start us, length us, event | category | flops | bytes accessed | tf_op | source)
XLA Modules:
  0.0 124.8 jit_solution(16484945545335845943)
XLA Ops:
  0.0 2.0 %shard_map.37 = bf16[32,2048]{1,0:T(8,128)(2,1)} custom-call(bf16[32,2048]{1,0:T(8,128)(2,1)} %rows_ref.1, bf16[16,128,128]{2,1,0:T(8,128)(2,1)} %precond_ref.1), custom_call_target="tpu_custom_call" | custom-call | tf_op jit(solution)/shard_map/pallas_call | solution.py:22
  2.0 4.4 %collective-permute-start = (bf16[32,2048]{1,0:T(8,128)(2,1)}, bf16[32,2048]{1,0:T(8,128)(2,1)S(1)}, u32[]{:S(2)}, u32[]{:S(2)}) collective-permute-start(bf16[32,2048]{1,0:T(8,128)(2,1)} %shard_map.37), channel_id=1, source_target_pairs={{0,128},{128,256},{256,384},{384,0},{1,129},{129,257},{257,385},{3... | collective-permute-start | bytes 393224 | tf_op jit(solution)/shard_map/ppermute | solution.py:32
  6.4 4.9 %collective-permute-start.1 = (bf16[32,2048]{1,0:T(8,128)(2,1)}, bf16[32,2048]{1,0:T(8,128)(2,1)S(1)}, u32[]{:S(2)}, u32[]{:S(2)}) collective-permute-start(bf16[32,2048]{1,0:T(8,128)(2,1)} %shard_map.37), channel_id=1, source_target_pairs={{0,256},{128,384},{256,0},{384,128},{1,257},{129,385},{257,1},{385... | collective-permute-start | bytes 393224 | tf_op jit(solution)/shard_map/ppermute | solution.py:32
  11.3 2.6 %collective-permute-start.2 = (bf16[32,2048]{1,0:T(8,128)(2,1)}, bf16[32,2048]{1,0:T(8,128)(2,1)S(1)}, u32[]{:S(2)}, u32[]{:S(2)}) collective-permute-start(bf16[32,2048]{1,0:T(8,128)(2,1)} %shard_map.37), channel_id=1, source_target_pairs={{0,384},{128,0},{256,128},{384,256},{1,385},{129,1},{257,129},{385... | collective-permute-start | bytes 393224 | tf_op jit(solution)/shard_map/ppermute | solution.py:32
  13.9 3.2 %collective-permute-start.3 = (bf16[32,2048]{1,0:T(8,128)(2,1)}, bf16[32,2048]{1,0:T(8,128)(2,1)S(1)}, u32[]{:S(2)}, u32[]{:S(2)}) collective-permute-start(bf16[32,2048]{1,0:T(8,128)(2,1)} %shard_map.37), channel_id=1, source_target_pairs={{0,32},{32,64},{64,96},{96,0},{1,33},{33,65},{65,97},{97,1},{2,34}... | collective-permute-start | bytes 393224 | tf_op jit(solution)/shard_map/ppermute | solution.py:32
  17.2 4.5 %collective-permute-start.4 = (bf16[32,2048]{1,0:T(8,128)(2,1)}, bf16[32,2048]{1,0:T(8,128)(2,1)S(1)}, u32[]{:S(2)}, u32[]{:S(2)}) collective-permute-start(bf16[32,2048]{1,0:T(8,128)(2,1)} %shard_map.37), channel_id=1, source_target_pairs={{0,64},{32,96},{64,0},{96,32},{1,65},{33,97},{65,1},{97,33},{2,66}... | collective-permute-start | bytes 393224 | tf_op jit(solution)/shard_map/ppermute | solution.py:32
  21.7 0.0 collective-permute-done
  21.7 3.0 %collective-permute-start.5 = (bf16[32,2048]{1,0:T(8,128)(2,1)}, bf16[32,2048]{1,0:T(8,128)(2,1)S(1)}, u32[]{:S(2)}, u32[]{:S(2)}) collective-permute-start(bf16[32,2048]{1,0:T(8,128)(2,1)} %shard_map.37), channel_id=1, source_target_pairs={{0,96},{32,0},{64,32},{96,64},{1,97},{33,1},{65,33},{97,65},{2,98}... | collective-permute-start | bytes 393224 | tf_op jit(solution)/shard_map/ppermute | solution.py:32
  24.7 0.9 constant_dynamic-update-slice_fusion.12
  25.6 0.0 collective-permute-done.1
  25.6 0.0 collective-permute-done.2
  25.6 0.0 collective-permute-done.3
  25.6 0.2 collective-permute-done.4
  25.8 2.3 %collective-permute-done.5 = bf16[32,2048]{1,0:T(8,128)(2,1)S(1)} collective-permute-done((bf16[32,2048]{1,0:T(8,128)(2,1)}, bf16[32,2048]{1,0:T(8,128)(2,1)S(1)}, u32[]{:S(2)}, u32[]{:S(2)}) %collective-permute-start.5) | collective-permute-done | bytes 131104 | tf_op jit(solution)/shard_map/ppermute | solution.py:32
  28.2 1.9 %collective-permute-start.6 = (bf16[96,2048]{1,0:T(8,128)(2,1)S(1)}, bf16[96,2048]{1,0:T(8,128)(2,1)S(1)}, u32[]{:S(2)}, u32[]{:S(2)}) collective-permute-start(bf16[96,2048]{1,0:T(8,128)(2,1)S(1)} %get-tuple-element.49), channel_id=1, source_target_pairs={{0,32},{32,64},{64,96},{96,0},{1,33},{33,65},{65,97},{97,1},{2,34}... | collective-permute-start | bytes 1179656 | tf_op jit(solution)/shard_map/ppermute | solution.py:32
  30.1 5.2 %collective-permute-start.7 = (bf16[96,2048]{1,0:T(8,128)(2,1)S(1)}, bf16[96,2048]{1,0:T(8,128)(2,1)S(1)}, u32[]{:S(2)}, u32[]{:S(2)}) collective-permute-start(bf16[96,2048]{1,0:T(8,128)(2,1)S(1)} %get-tuple-element.49), channel_id=1, source_target_pairs={{0,64},{32,96},{64,0},{96,32},{1,65},{33,97},{65,1},{97,33},{2,66}... | collective-permute-start | bytes 1179656 | tf_op jit(solution)/shard_map/ppermute | solution.py:32
  35.3 2.0 %collective-permute-start.8 = (bf16[96,2048]{1,0:T(8,128)(2,1)S(1)}, bf16[96,2048]{1,0:T(8,128)(2,1)S(1)}, u32[]{:S(2)}, u32[]{:S(2)}) collective-permute-start(bf16[96,2048]{1,0:T(8,128)(2,1)S(1)} %get-tuple-element.49), channel_id=1, source_target_pairs={{0,96},{32,0},{64,32},{96,64},{1,97},{33,1},{65,33},{97,65},{2,98}... | collective-permute-start | bytes 1179656 | tf_op jit(solution)/shard_map/ppermute | solution.py:32
  37.3 1.2 collective-permute-done.6
  38.5 9.1 %collective-permute-done.7 = bf16[96,2048]{1,0:T(8,128)(2,1)S(1)} collective-permute-done((bf16[96,2048]{1,0:T(8,128)(2,1)S(1)}, bf16[96,2048]{1,0:T(8,128)(2,1)S(1)}, u32[]{:S(2)}, u32[]{:S(2)}) %collective-permute-start.7) | collective-permute-done | bytes 393248 | tf_op jit(solution)/shard_map/ppermute | solution.py:32
  47.7 3.0 %collective-permute-done.8 = bf16[96,2048]{1,0:T(8,128)(2,1)S(1)} collective-permute-done((bf16[96,2048]{1,0:T(8,128)(2,1)S(1)}, bf16[96,2048]{1,0:T(8,128)(2,1)S(1)}, u32[]{:S(2)}, u32[]{:S(2)}) %collective-permute-start.8) | collective-permute-done | bytes 393248 | tf_op jit(solution)/shard_map/ppermute | solution.py:32
  50.8 4.9 %collective-permute-start.9 = (bf16[512,2048]{1,0:T(8,128)(2,1)S(1)}, bf16[512,2048]{1,0:T(8,128)(2,1)}, u32[]{:S(2)}, u32[]{:S(2)}) collective-permute-start(bf16[512,2048]{1,0:T(8,128)(2,1)S(1)} %constant_dynamic-update-slice_fusion.3), channel_id=1, source_target_pairs={{0,16},{16,0},{1,17},{17,1},{2,18},{18,2},{3,19},{19,3},{4,20},{20... | collective-permute-start | bytes 6291464 | tf_op jit(solution)/shard_map/ppermute | solution.py:32
  55.9 0.0 copy-start
  55.9 4.7 %convolution_convert_fusion.1 = bf16[512,1024]{1,0:T(8,128)(2,1)S(1)} fusion(bf16[512,2048]{1,0:T(8,128)(2,1)S(1)} %constant_dynamic-update-slice_fusion.3, bf16[1024,2048]{1,0:T(8,128)(2,1)} %param.3), kind=kOutput, calls=%fused_computation.1 | convolution fusion | flops 2148007936 | bytes 7340032 | tf_op jit(solution)/shard_map/dot_general | solution.py:36
  60.6 0.0 collective-permute-done.9
  60.6 0.0 copy-done
  60.6 4.0 %convolution_convert_fusion = bf16[512,1024]{1,0:T(8,128)(2,1)S(1)} fusion(bf16[512,2048]{1,0:T(8,128)(2,1)} %collective-permute-done.9, bf16[1024,2048]{1,0:T(8,128)(2,1)S(1)} %copy-done), kind=kOutput, calls=%fused_computation | convolution fusion | flops 2148007936 | bytes 7340032 | tf_op jit(solution)/shard_map/dot_general | solution.py:36
  64.6 0.4 dynamic-slice_bitcast_fusion.30
  65.1 3.9 %collective-permute-start.10 = (bf16[4,32,1024]{2,1,0:T(8,128)(2,1)S(1)}, bf16[4,32,1024]{2,1,0:T(8,128)(2,1)S(1)}, u32[]{:S(2)}, u32[]{:S(2)}) collective-permute-start(bf16[4,32,1024]{2,1,0:T(8,128)(2,1)S(1)} %pad_maximum_fusion), channel_id=1, source_target_pairs={{0,4},{4,0},{8,12},{12,8},{16,28},{20,24},{24,20},{28,16},{1,5},{5... | collective-permute-start | bytes 786440 | tf_op jit(solution)/shard_map/ppermute | solution.py:48
  69.0 2.6 %collective-permute-start.12 = (bf16[4,32,1024]{2,1,0:T(8,128)(2,1)S(1)}, bf16[4,32,1024]{2,1,0:T(8,128)(2,1)S(1)}, u32[]{:S(2)}, u32[]{:S(2)}) collective-permute-start(bf16[4,32,1024]{2,1,0:T(8,128)(2,1)S(1)} %pad_maximum_fusion.1), channel_id=1, source_target_pairs={{0,4},{4,0},{8,12},{12,8},{16,28},{20,24},{24,20},{28,16},{1,5},{5... | collective-permute-start | bytes 786440 | tf_op jit(solution)/shard_map/ppermute | solution.py:48
  71.7 3.9 %collective-permute-start.15 = (bf16[4,32,1024]{2,1,0:T(8,128)(2,1)S(1)}, bf16[4,32,1024]{2,1,0:T(8,128)(2,1)S(1)}, u32[]{:S(2)}, u32[]{:S(2)}) collective-permute-start(bf16[4,32,1024]{2,1,0:T(8,128)(2,1)S(1)} %pad_maximum_fusion.2), channel_id=1, source_target_pairs={{0,4},{4,0},{8,12},{12,8},{16,28},{20,24},{24,20},{28,16},{1,5},{5... | collective-permute-start | bytes 786440 | tf_op jit(solution)/shard_map/ppermute | solution.py:48
  75.6 2.6 %collective-permute-start.18 = (bf16[4,32,1024]{2,1,0:T(8,128)(2,1)S(1)}, bf16[4,32,1024]{2,1,0:T(8,128)(2,1)S(1)}, u32[]{:S(2)}, u32[]{:S(2)}) collective-permute-start(bf16[4,32,1024]{2,1,0:T(8,128)(2,1)S(1)} %pad_maximum_fusion.3), channel_id=1, source_target_pairs={{0,4},{4,0},{8,12},{12,8},{16,28},{20,24},{24,20},{28,16},{1,5},{5... | collective-permute-start | bytes 786440 | tf_op jit(solution)/shard_map/ppermute | solution.py:48
  78.2 0.0 collective-permute-done.10
  78.3 1.9 %collective-permute-start.11 = (bf16[2,32,1024]{2,1,0:T(8,128)(2,1)S(1)}, bf16[2,32,1024]{2,1,0:T(8,128)(2,1)S(1)}, u32[]{:S(2)}, u32[]{:S(2)}) collective-permute-start(bf16[2,32,1024]{2,1,0:T(8,128)(2,1)S(1)} %add_convert_fusion.7), channel_id=1, source_target_pairs={{0,12},{4,8},{8,4},{12,0},{16,20},{20,16},{24,28},{28,24},{1,13},{... | collective-permute-start | bytes 393224 | tf_op jit(solution)/shard_map/ppermute | solution.py:48
  80.2 0.0 collective-permute-done.12
  80.3 3.4 %collective-permute-start.13 = (bf16[2,32,1024]{2,1,0:T(8,128)(2,1)S(1)}, bf16[2,32,1024]{2,1,0:T(8,128)(2,1)S(1)}, u32[]{:S(2)}, u32[]{:S(2)}) collective-permute-start(bf16[2,32,1024]{2,1,0:T(8,128)(2,1)S(1)} %add_convert_fusion.6), channel_id=1, source_target_pairs={{0,12},{4,8},{8,4},{12,0},{16,20},{20,16},{24,28},{28,24},{1,13},{... | collective-permute-start | bytes 393224 | tf_op jit(solution)/shard_map/ppermute | solution.py:48
  83.6 0.0 collective-permute-done.15
  83.7 1.9 %collective-permute-start.16 = (bf16[2,32,1024]{2,1,0:T(8,128)(2,1)S(1)}, bf16[2,32,1024]{2,1,0:T(8,128)(2,1)S(1)}, u32[]{:S(2)}, u32[]{:S(2)}) collective-permute-start(bf16[2,32,1024]{2,1,0:T(8,128)(2,1)S(1)} %add_convert_fusion.4), channel_id=1, source_target_pairs={{0,12},{4,8},{8,4},{12,0},{16,20},{20,16},{24,28},{28,24},{1,13},{... | collective-permute-start | bytes 393224 | tf_op jit(solution)/shard_map/ppermute | solution.py:48
  85.6 0.0 collective-permute-done.18
  85.7 3.4 %collective-permute-start.19 = (bf16[2,32,1024]{2,1,0:T(8,128)(2,1)S(1)}, bf16[2,32,1024]{2,1,0:T(8,128)(2,1)S(1)}, u32[]{:S(2)}, u32[]{:S(2)}) collective-permute-start(bf16[2,32,1024]{2,1,0:T(8,128)(2,1)S(1)} %add_convert_fusion.2), channel_id=1, source_target_pairs={{0,12},{4,8},{8,4},{12,0},{16,20},{20,16},{24,28},{28,24},{1,13},{... | collective-permute-start | bytes 393224 | tf_op jit(solution)/shard_map/ppermute | solution.py:48
  89.0 0.0 collective-permute-done.13
  89.0 0.1 add_convert_fusion.5
  89.1 13.1 %collective-permute-start.14 = (bf16[2,32,1024]{2,1,0:T(8,128)(2,1)S(1)}, bf16[2,32,1024]{2,1,0:T(8,128)(2,1)S(1)}, u32[]{:S(2)}, u32[]{:S(2)}) collective-permute-start(bf16[2,32,1024]{2,1,0:T(8,128)(2,1)S(1)} %add_convert_fusion.5), channel_id=1, source_target_pairs={{0,2},{1,3},{2,0},{3,1},{4,6},{5,7},{6,4},{7,5},{8,10},{9,11},{10,... | collective-permute-start | bytes 393224 | tf_op jit(solution)/shard_map/ppermute | solution.py:32
  102.3 0.0 collective-permute-done.16
  102.3 0.1 add_convert_fusion.3
  102.3 4.0 %collective-permute-start.17 = (bf16[2,32,1024]{2,1,0:T(8,128)(2,1)S(1)}, bf16[2,32,1024]{2,1,0:T(8,128)(2,1)S(1)}, u32[]{:S(2)}, u32[]{:S(2)}) collective-permute-start(bf16[2,32,1024]{2,1,0:T(8,128)(2,1)S(1)} %add_convert_fusion.3), channel_id=1, source_target_pairs={{0,1},{1,2},{2,3},{3,0},{4,5},{5,6},{6,7},{7,4},{8,9},{9,10},{10,1... | collective-permute-start | bytes 393224 | tf_op jit(solution)/shard_map/ppermute | solution.py:32
  106.3 0.0 collective-permute-done.19
  106.4 0.1 add_convert_fusion.1
  106.4 5.2 %collective-permute-start.20 = (bf16[2,32,1024]{2,1,0:T(8,128)(2,1)S(1)}, bf16[2,32,1024]{2,1,0:T(8,128)(2,1)S(1)}, u32[]{:S(2)}, u32[]{:S(2)}) collective-permute-start(bf16[2,32,1024]{2,1,0:T(8,128)(2,1)S(1)} %add_convert_fusion.1), channel_id=1, source_target_pairs={{0,3},{1,0},{2,1},{3,2},{4,7},{5,4},{6,5},{7,6},{8,11},{9,8},{10,9... | collective-permute-start | bytes 393224 | tf_op jit(solution)/shard_map/ppermute | solution.py:32
  111.6 0.0 collective-permute-done.11
  111.6 0.0 collective-permute-done.14
  111.6 11.2 %collective-permute-done.17 = bf16[2,32,1024]{2,1,0:T(8,128)(2,1)S(1)} collective-permute-done((bf16[2,32,1024]{2,1,0:T(8,128)(2,1)S(1)}, bf16[2,32,1024]{2,1,0:T(8,128)(2,1)S(1)}, u32[]{:S(2)}, u32[]{:S(2)}) %collective-permute-start.17) | collective-permute-done | bytes 131104 | tf_op jit(solution)/shard_map/ppermute | solution.py:32
  122.9 1.1 collective-permute-done.20
  124.0 0.1 add_convert_fusion
  124.1 0.7 reverse_select_fusion
  (17 shorter events, 0.5 us)
Async XLA Ops:
  2.0 19.7 %collective-permute-start = (bf16[32,2048]{1,0:T(8,128)(2,1)}, bf16[32,2048]{1,0:T(8,128)(2,1)S(1)}, u32[]{:S(2)}, u32[]{:S(2)}) collective-permute-start(bf16[32,2048]{1,0:T(8,128)(2,1)} %shard_map.37), channel_id=1, source_target_pairs={{0,128},{128,256},{256,384},{384,0},{1,129},{129,257},{257,385},{3... | collective-permute-start | bytes 393224 | tf_op jit(solution)/shard_map/ppermute | solution.py:32
  6.4 19.2 %collective-permute-start.1 = (bf16[32,2048]{1,0:T(8,128)(2,1)}, bf16[32,2048]{1,0:T(8,128)(2,1)S(1)}, u32[]{:S(2)}, u32[]{:S(2)}) collective-permute-start(bf16[32,2048]{1,0:T(8,128)(2,1)} %shard_map.37), channel_id=1, source_target_pairs={{0,256},{128,384},{256,0},{384,128},{1,257},{129,385},{257,1},{385... | collective-permute-start | bytes 393224 | tf_op jit(solution)/shard_map/ppermute | solution.py:32
  11.3 14.3 %collective-permute-start.2 = (bf16[32,2048]{1,0:T(8,128)(2,1)}, bf16[32,2048]{1,0:T(8,128)(2,1)S(1)}, u32[]{:S(2)}, u32[]{:S(2)}) collective-permute-start(bf16[32,2048]{1,0:T(8,128)(2,1)} %shard_map.37), channel_id=1, source_target_pairs={{0,384},{128,0},{256,128},{384,256},{1,385},{129,1},{257,129},{385... | collective-permute-start | bytes 393224 | tf_op jit(solution)/shard_map/ppermute | solution.py:32
  13.9 11.7 %collective-permute-start.3 = (bf16[32,2048]{1,0:T(8,128)(2,1)}, bf16[32,2048]{1,0:T(8,128)(2,1)S(1)}, u32[]{:S(2)}, u32[]{:S(2)}) collective-permute-start(bf16[32,2048]{1,0:T(8,128)(2,1)} %shard_map.37), channel_id=1, source_target_pairs={{0,32},{32,64},{64,96},{96,0},{1,33},{33,65},{65,97},{97,1},{2,34}... | collective-permute-start | bytes 393224 | tf_op jit(solution)/shard_map/ppermute | solution.py:32
  17.2 8.6 %collective-permute-start.4 = (bf16[32,2048]{1,0:T(8,128)(2,1)}, bf16[32,2048]{1,0:T(8,128)(2,1)S(1)}, u32[]{:S(2)}, u32[]{:S(2)}) collective-permute-start(bf16[32,2048]{1,0:T(8,128)(2,1)} %shard_map.37), channel_id=1, source_target_pairs={{0,64},{32,96},{64,0},{96,32},{1,65},{33,97},{65,1},{97,33},{2,66}... | collective-permute-start | bytes 393224 | tf_op jit(solution)/shard_map/ppermute | solution.py:32
  21.7 6.4 %collective-permute-start.5 = (bf16[32,2048]{1,0:T(8,128)(2,1)}, bf16[32,2048]{1,0:T(8,128)(2,1)S(1)}, u32[]{:S(2)}, u32[]{:S(2)}) collective-permute-start(bf16[32,2048]{1,0:T(8,128)(2,1)} %shard_map.37), channel_id=1, source_target_pairs={{0,96},{32,0},{64,32},{96,64},{1,97},{33,1},{65,33},{97,65},{2,98}... | collective-permute-start | bytes 393224 | tf_op jit(solution)/shard_map/ppermute | solution.py:32
  28.2 10.3 %collective-permute-start.6 = (bf16[96,2048]{1,0:T(8,128)(2,1)S(1)}, bf16[96,2048]{1,0:T(8,128)(2,1)S(1)}, u32[]{:S(2)}, u32[]{:S(2)}) collective-permute-start(bf16[96,2048]{1,0:T(8,128)(2,1)S(1)} %get-tuple-element.49), channel_id=1, source_target_pairs={{0,32},{32,64},{64,96},{96,0},{1,33},{33,65},{65,97},{97,1},{2,34}... | collective-permute-start | bytes 1179656 | tf_op jit(solution)/shard_map/ppermute | solution.py:32
  30.1 17.6 %collective-permute-start.7 = (bf16[96,2048]{1,0:T(8,128)(2,1)S(1)}, bf16[96,2048]{1,0:T(8,128)(2,1)S(1)}, u32[]{:S(2)}, u32[]{:S(2)}) collective-permute-start(bf16[96,2048]{1,0:T(8,128)(2,1)S(1)} %get-tuple-element.49), channel_id=1, source_target_pairs={{0,64},{32,96},{64,0},{96,32},{1,65},{33,97},{65,1},{97,33},{2,66}... | collective-permute-start | bytes 1179656 | tf_op jit(solution)/shard_map/ppermute | solution.py:32
  35.3 15.4 %collective-permute-start.8 = (bf16[96,2048]{1,0:T(8,128)(2,1)S(1)}, bf16[96,2048]{1,0:T(8,128)(2,1)S(1)}, u32[]{:S(2)}, u32[]{:S(2)}) collective-permute-start(bf16[96,2048]{1,0:T(8,128)(2,1)S(1)} %get-tuple-element.49), channel_id=1, source_target_pairs={{0,96},{32,0},{64,32},{96,64},{1,97},{33,1},{65,33},{97,65},{2,98}... | collective-permute-start | bytes 1179656 | tf_op jit(solution)/shard_map/ppermute | solution.py:32
  50.8 9.8 %collective-permute-start.9 = (bf16[512,2048]{1,0:T(8,128)(2,1)S(1)}, bf16[512,2048]{1,0:T(8,128)(2,1)}, u32[]{:S(2)}, u32[]{:S(2)}) collective-permute-start(bf16[512,2048]{1,0:T(8,128)(2,1)S(1)} %constant_dynamic-update-slice_fusion.3), channel_id=1, source_target_pairs={{0,16},{16,0},{1,17},{17,1},{2,18},{18,2},{3,19},{19,3},{4,20},{20... | collective-permute-start | bytes 6291464 | tf_op jit(solution)/shard_map/ppermute | solution.py:32
  55.9 4.7 %copy-start = (bf16[1024,2048]{1,0:T(8,128)(2,1)S(1)}, bf16[1024,2048]{1,0:T(8,128)(2,1)}, u32[]{:S(2)}) copy-start(bf16[1024,2048]{1,0:T(8,128)(2,1)} %param.3) | copy-start | bytes 12582916
  65.1 13.2 %collective-permute-start.10 = (bf16[4,32,1024]{2,1,0:T(8,128)(2,1)S(1)}, bf16[4,32,1024]{2,1,0:T(8,128)(2,1)S(1)}, u32[]{:S(2)}, u32[]{:S(2)}) collective-permute-start(bf16[4,32,1024]{2,1,0:T(8,128)(2,1)S(1)} %pad_maximum_fusion), channel_id=1, source_target_pairs={{0,4},{4,0},{8,12},{12,8},{16,28},{20,24},{24,20},{28,16},{1,5},{5... | collective-permute-start | bytes 786440 | tf_op jit(solution)/shard_map/ppermute | solution.py:48
  69.0 11.2 %collective-permute-start.12 = (bf16[4,32,1024]{2,1,0:T(8,128)(2,1)S(1)}, bf16[4,32,1024]{2,1,0:T(8,128)(2,1)S(1)}, u32[]{:S(2)}, u32[]{:S(2)}) collective-permute-start(bf16[4,32,1024]{2,1,0:T(8,128)(2,1)S(1)} %pad_maximum_fusion.1), channel_id=1, source_target_pairs={{0,4},{4,0},{8,12},{12,8},{16,28},{20,24},{24,20},{28,16},{1,5},{5... | collective-permute-start | bytes 786440 | tf_op jit(solution)/shard_map/ppermute | solution.py:48
  71.7 12.0 %collective-permute-start.15 = (bf16[4,32,1024]{2,1,0:T(8,128)(2,1)S(1)}, bf16[4,32,1024]{2,1,0:T(8,128)(2,1)S(1)}, u32[]{:S(2)}, u32[]{:S(2)}) collective-permute-start(bf16[4,32,1024]{2,1,0:T(8,128)(2,1)S(1)} %pad_maximum_fusion.2), channel_id=1, source_target_pairs={{0,4},{4,0},{8,12},{12,8},{16,28},{20,24},{24,20},{28,16},{1,5},{5... | collective-permute-start | bytes 786440 | tf_op jit(solution)/shard_map/ppermute | solution.py:48
  75.6 10.0 %collective-permute-start.18 = (bf16[4,32,1024]{2,1,0:T(8,128)(2,1)S(1)}, bf16[4,32,1024]{2,1,0:T(8,128)(2,1)S(1)}, u32[]{:S(2)}, u32[]{:S(2)}) collective-permute-start(bf16[4,32,1024]{2,1,0:T(8,128)(2,1)S(1)} %pad_maximum_fusion.3), channel_id=1, source_target_pairs={{0,4},{4,0},{8,12},{12,8},{16,28},{20,24},{24,20},{28,16},{1,5},{5... | collective-permute-start | bytes 786440 | tf_op jit(solution)/shard_map/ppermute | solution.py:48
  78.3 33.3 %collective-permute-start.11 = (bf16[2,32,1024]{2,1,0:T(8,128)(2,1)S(1)}, bf16[2,32,1024]{2,1,0:T(8,128)(2,1)S(1)}, u32[]{:S(2)}, u32[]{:S(2)}) collective-permute-start(bf16[2,32,1024]{2,1,0:T(8,128)(2,1)S(1)} %add_convert_fusion.7), channel_id=1, source_target_pairs={{0,12},{4,8},{8,4},{12,0},{16,20},{20,16},{24,28},{28,24},{1,13},{... | collective-permute-start | bytes 393224 | tf_op jit(solution)/shard_map/ppermute | solution.py:48
  80.3 8.8 %collective-permute-start.13 = (bf16[2,32,1024]{2,1,0:T(8,128)(2,1)S(1)}, bf16[2,32,1024]{2,1,0:T(8,128)(2,1)S(1)}, u32[]{:S(2)}, u32[]{:S(2)}) collective-permute-start(bf16[2,32,1024]{2,1,0:T(8,128)(2,1)S(1)} %add_convert_fusion.6), channel_id=1, source_target_pairs={{0,12},{4,8},{8,4},{12,0},{16,20},{20,16},{24,28},{28,24},{1,13},{... | collective-permute-start | bytes 393224 | tf_op jit(solution)/shard_map/ppermute | solution.py:48
  83.7 18.6 %collective-permute-start.16 = (bf16[2,32,1024]{2,1,0:T(8,128)(2,1)S(1)}, bf16[2,32,1024]{2,1,0:T(8,128)(2,1)S(1)}, u32[]{:S(2)}, u32[]{:S(2)}) collective-permute-start(bf16[2,32,1024]{2,1,0:T(8,128)(2,1)S(1)} %add_convert_fusion.4), channel_id=1, source_target_pairs={{0,12},{4,8},{8,4},{12,0},{16,20},{20,16},{24,28},{28,24},{1,13},{... | collective-permute-start | bytes 393224 | tf_op jit(solution)/shard_map/ppermute | solution.py:48
  85.7 20.7 %collective-permute-start.19 = (bf16[2,32,1024]{2,1,0:T(8,128)(2,1)S(1)}, bf16[2,32,1024]{2,1,0:T(8,128)(2,1)S(1)}, u32[]{:S(2)}, u32[]{:S(2)}) collective-permute-start(bf16[2,32,1024]{2,1,0:T(8,128)(2,1)S(1)} %add_convert_fusion.2), channel_id=1, source_target_pairs={{0,12},{4,8},{8,4},{12,0},{16,20},{20,16},{24,28},{28,24},{1,13},{... | collective-permute-start | bytes 393224 | tf_op jit(solution)/shard_map/ppermute | solution.py:48
  89.1 22.5 %collective-permute-start.14 = (bf16[2,32,1024]{2,1,0:T(8,128)(2,1)S(1)}, bf16[2,32,1024]{2,1,0:T(8,128)(2,1)S(1)}, u32[]{:S(2)}, u32[]{:S(2)}) collective-permute-start(bf16[2,32,1024]{2,1,0:T(8,128)(2,1)S(1)} %add_convert_fusion.5), channel_id=1, source_target_pairs={{0,2},{1,3},{2,0},{3,1},{4,6},{5,7},{6,4},{7,5},{8,10},{9,11},{10,... | collective-permute-start | bytes 393224 | tf_op jit(solution)/shard_map/ppermute | solution.py:32
  102.3 20.5 %collective-permute-start.17 = (bf16[2,32,1024]{2,1,0:T(8,128)(2,1)S(1)}, bf16[2,32,1024]{2,1,0:T(8,128)(2,1)S(1)}, u32[]{:S(2)}, u32[]{:S(2)}) collective-permute-start(bf16[2,32,1024]{2,1,0:T(8,128)(2,1)S(1)} %add_convert_fusion.3), channel_id=1, source_target_pairs={{0,1},{1,2},{2,3},{3,0},{4,5},{5,6},{6,7},{7,4},{8,9},{9,10},{10,1... | collective-permute-start | bytes 393224 | tf_op jit(solution)/shard_map/ppermute | solution.py:32
  106.4 17.6 %collective-permute-start.20 = (bf16[2,32,1024]{2,1,0:T(8,128)(2,1)S(1)}, bf16[2,32,1024]{2,1,0:T(8,128)(2,1)S(1)}, u32[]{:S(2)}, u32[]{:S(2)}) collective-permute-start(bf16[2,32,1024]{2,1,0:T(8,128)(2,1)S(1)} %add_convert_fusion.1), channel_id=1, source_target_pairs={{0,3},{1,0},{2,1},{3,2},{4,7},{5,4},{6,5},{7,6},{8,11},{9,8},{10,9... | collective-permute-start | bytes 393224 | tf_op jit(solution)/shard_map/ppermute | solution.py:32

commit v3 on v1

--- a/solution.py
+++ b/solution.py
@@ -1,6 +1,5 @@
 import jax
 import jax.numpy as jnp
-import numpy as np
 from jax import lax
 from jax.experimental import pallas as pl
 from jax.experimental.pallas import tpu as pltpu
@@ -40,11 +39,22 @@
     return out.astype(jnp.bfloat16)
 
 
-def f32_sum(arrays):
-    total = arrays[0].astype(jnp.float32)
-    for a in arrays[1:]:
-        total = total + a.astype(jnp.float32)
-    return total
+def halve(array, axis, first):
+    names = {"y": ("y", "core"), "x": ("core", "x"), "zh": ("core", "zh")}[axis]
+    pairs = []
+    for core in range(2):
+        for i in range(4):
+            up = (i + core + (0 if first else 1)) % 2 == 0
+            to = (i + (1 if up else 3)) % 4
+            if axis == "y":
+                pairs.append((i * 2 + core, to * 2 + core))
+            else:
+                pairs.append((core * 4 + i, core * 4 + to))
+    return lax.ppermute(array, names, pairs)
+
+
+def first_step(index, core):
+    return jnp.where(jnp.mod(index + core, 2) == 0, 1, 3)
 
 
 def per_device(train_grads, test_grads, precond):
@@ -53,29 +63,51 @@
     count = test_grads.shape[0]
     width = train_grads.shape[0]
 
+    even_y = jnp.mod(y + core, 2) == 0
+    step_x, step_zh = first_step(x, core), first_step(zh, core)
+
     own = condition(test_grads, precond)
-    line = jnp.concatenate([own] + [shift(own, "zl", k) for k in (1, 2, 3)], axis=0)
-    plane = jnp.concatenate([line] + [shift(line, "y", m) for m in (1, 2, 3)], axis=0)
-    other = shift(plane, "core", 1)
+    line = [own] + [shift(own, "zl", k) for k in (1, 2, 3)]
 
-    shape = (4, 4, count, width)
-    part = [dot_t(plane, train_grads).reshape(shape), dot_t(other, train_grads).reshape(shape)]
+    def partials(pieces):
+        rows = jnp.concatenate(pieces, axis=0)
+        rows = jnp.concatenate([rows, halve(rows, "y", True)], axis=0)
+        rows = jnp.concatenate([rows, halve(rows, "y", False)], axis=0)
+        both = [rows, lax.ppermute(rows, "core", [(0, 1), (1, 0)])]
+        return [dot_t(r, train_grads).reshape(4, 2, count, width) for r in both]
 
-    def for_x(step):
-        k = jnp.mod(zl - x - step, 4)
-        return jnp.stack(
-            [lax.dynamic_index_in_dim(p, k, axis=1, keepdims=False) for p in part], axis=1
-        )
+    parts = [partials(line[:2]), partials(line[2:])]
 
-    got = [for_x(0)] + [shift(for_x(j), "x", j) for j in (1, 2, 3)]
-    total = f32_sum(got)
+    def block(home_x, home_zh):
+        k = jnp.mod(zl - home_x, 4)
+        d = jnp.mod(home_zh - y, 4)
+        up = jnp.where(d < 2, d, 5 - d)
+        down = jnp.where(d == 0, 0, jnp.where(d == 2, 3, jnp.where(d == 1, 2, 1)))
+        m = [jnp.where(even_y, up, down), jnp.where(even_y, down, up)]
+        found = [
+            [
+                lax.dynamic_slice(part[c], (m[c], jnp.mod(k, 2), 0, 0), (1, 1, count, width))[0, 0]
+                for part in parts
+            ]
+            for c in range(2)
+        ]
+        return jnp.concatenate([jnp.where(k < 2, *f) for f in found], axis=0)
 
-    def for_zh(step):
-        m = jnp.mod(y - zh - step, 4)
-        return lax.dynamic_index_in_dim(total, m, axis=0, keepdims=False)
+    def sum_x(homes):
+        def blocks(home_x):
+            return jnp.stack([block(home_x, home) for home in homes])
 
-    last = [for_zh(0)] + [shift(for_zh(i).astype(jnp.bfloat16), "zh", i) for i in (1, 2, 3)]
-    scores = f32_sum(last).astype(jnp.bfloat16)
+        send = jnp.stack([blocks(x + step_x), blocks(x + 2)])
+        got = halve(send, "x", True).astype(jnp.float32)
+        keep = blocks(x).astype(jnp.float32) + got[0]
+        back = blocks(x - step_x).astype(jnp.float32) + got[1]
+        return keep + halve(back.astype(jnp.bfloat16), "x", False).astype(jnp.float32)
+
+    far = sum_x([zh + step_zh, zh + 2])
+    near = sum_x([zh, zh - step_zh])
+    near = near + halve(far.astype(jnp.bfloat16), "zh", True).astype(jnp.float32)
+    last = halve(near[1].astype(jnp.bfloat16), "zh", False).astype(jnp.float32)
+    scores = (near[0] + last).astype(jnp.bfloat16).reshape(2, count, width)
     scores = jnp.where(core == 0, scores, scores[::-1])
     return scores.reshape(2 * count, width)
 

time: 138 us -> 111 us (0.80)
  the two profiles are of different devices: /device:TPU:105 before, /device:TPU:40 now
where the time goes in v3:
time: 111 us
  starting transfers between devices  60.6 us (55%)
  waiting for transfers between devices  38.7 us (35%)
  matrix products  5.13 us (5%)
  other arithmetic  3.22 us (3%)
  Pallas kernels  2.02 us (2%)
    ppermute x10, starting transfers between devices, halve(): return lax.ppermute(array, names, pairs)  45.6 us
    ppermute x10, waiting for transfers between devices, halve(): return lax.ppermute(array, names, pairs)  36.6 us
    ppermute x3, starting transfers between devices, shift(): lax.ppermute(array, axis, [(i, (i + step) % size) for i in range(size)])  11.1 us
    dot_general x4, matrix products, dot_t(): lax.dot_general(rows, train, (((1,), (1,)), ((), ())), preferred_element_...  5.13 us
    ppermute x2, starting transfers between devices, partials(): both = [rows, lax.ppermute(rows, 'core', [(0, 1), (1, 0)])]  3.84 us
  transfers between devices with their start and end apart: 15, of which 9 were waited for; matrix products, arithmetic and copies ran while one was open for 5% of the time, Pallas kernels for 0%

profile of v3, /device:TPU:40, one launch (start us, length us, event | category | flops | bytes accessed | tf_op | source)
XLA Modules:
  0.0 110.6 jit_solution(14286999252452032649)
XLA Ops:
  0.0 2.0 %shard_map.37 = bf16[32,2048]{1,0:T(8,128)(2,1)} custom-call(bf16[32,2048]{1,0:T(8,128)(2,1)} %rows_ref.1, bf16[16,128,128]{2,1,0:T(8,128)(2,1)} %precond_ref.1), custom_call_target="tpu_custom_call" | custom-call | tf_op jit(solution)/shard_map/pallas_call | solution.py:22
  2.0 0.0 copy-start
  2.0 5.3 %collective-permute-start.3 = (bf16[32,2048]{1,0:T(8,128)(2,1)}, bf16[32,2048]{1,0:T(8,128)(2,1)S(1)}, u32[]{:S(2)}, u32[]{:S(2)}) collective-permute-start(bf16[32,2048]{1,0:T(8,128)(2,1)} %shard_map.37), channel_id=1, source_target_pairs={{0,256},{128,384},{256,0},{384,128},{1,257},{129,385},{257,1},{385... | collective-permute-start | bytes 393224 | tf_op jit(solution)/shard_map/ppermute | solution.py:32
  7.3 2.0 %collective-permute-start.4 = (bf16[32,2048]{1,0:T(8,128)(2,1)}, bf16[32,2048]{1,0:T(8,128)(2,1)S(1)}, u32[]{:S(2)}, u32[]{:S(2)}) collective-permute-start(bf16[32,2048]{1,0:T(8,128)(2,1)} %shard_map.37), channel_id=1, source_target_pairs={{0,384},{128,0},{256,128},{384,256},{1,385},{129,1},{257,129},{385... | collective-permute-start | bytes 393224 | tf_op jit(solution)/shard_map/ppermute | solution.py:32
  9.4 3.8 %collective-permute-start = (bf16[32,2048]{1,0:T(8,128)(2,1)}, bf16[32,2048]{1,0:T(8,128)(2,1)S(1)}, u32[]{:S(2)}, u32[]{:S(2)}) collective-permute-start(bf16[32,2048]{1,0:T(8,128)(2,1)} %shard_map.37), channel_id=1, source_target_pairs={{0,128},{128,256},{256,384},{384,0},{1,129},{129,257},{257,385},{3... | collective-permute-start | bytes 393224 | tf_op jit(solution)/shard_map/ppermute | solution.py:32
  13.6 2.1 %collective-permute-done.3 = bf16[32,2048]{1,0:T(8,128)(2,1)S(1)} collective-permute-done((bf16[32,2048]{1,0:T(8,128)(2,1)}, bf16[32,2048]{1,0:T(8,128)(2,1)S(1)}, u32[]{:S(2)}, u32[]{:S(2)}) %collective-permute-start.3) | collective-permute-done | bytes 131104 | tf_op jit(solution)/shard_map/ppermute | solution.py:32
  15.7 0.0 collective-permute-done.4
  15.7 4.1 %collective-permute-start.5 = (bf16[64,2048]{1,0:T(8,128)(2,1)S(1)}, bf16[64,2048]{1,0:T(8,128)(2,1)S(1)}, u32[]{:S(2)}, u32[]{:S(2)}) collective-permute-start(bf16[64,2048]{1,0:T(8,128)(2,1)S(1)} %pad_maximum_fusion.6), channel_id=1, source_target_pairs={{0,32},{32,0},{64,96},{96,64},{16,112},{48,80},{80,48},{112,16},{1... | collective-permute-start | bytes 786440 | tf_op jit(solution)/shard_map/ppermute | solution.py:53
  19.9 0.0 collective-permute-done
  19.9 0.9 pad_maximum_fusion.5
  20.8 1.9 %collective-permute-start.1 = (bf16[64,2048]{1,0:T(8,128)(2,1)S(1)}, bf16[64,2048]{1,0:T(8,128)(2,1)S(1)}, u32[]{:S(2)}, u32[]{:S(2)}) collective-permute-start(bf16[64,2048]{1,0:T(8,128)(2,1)S(1)} %pad_maximum_fusion.5), channel_id=1, source_target_pairs={{0,32},{32,0},{64,96},{96,64},{16,112},{48,80},{80,48},{112,16},{1... | collective-permute-start | bytes 786440 | tf_op jit(solution)/shard_map/ppermute | solution.py:53
  22.7 1.5 %collective-permute-done.5 = bf16[64,2048]{1,0:T(8,128)(2,1)S(1)} collective-permute-done((bf16[64,2048]{1,0:T(8,128)(2,1)S(1)}, bf16[64,2048]{1,0:T(8,128)(2,1)S(1)}, u32[]{:S(2)}, u32[]{:S(2)}) %collective-permute-start.5) | collective-permute-done | bytes 262176 | tf_op jit(solution)/shard_map/ppermute | solution.py:53
  24.2 3.3 %collective-permute-start.6 = (bf16[128,2048]{1,0:T(8,128)(2,1)S(1)}, bf16[128,2048]{1,0:T(8,128)(2,1)S(1)}, u32[]{:S(2)}, u32[]{:S(2)}) collective-permute-start(bf16[128,2048]{1,0:T(8,128)(2,1)S(1)} %pad_maximum_fusion.2), channel_id=1, source_target_pairs={{0,96},{32,64},{64,32},{96,0},{16,48},{48,16},{80,112},{112,80},{1... | collective-permute-start | bytes 1572872 | tf_op jit(solution)/shard_map/ppermute | solution.py:53
  27.5 3.0 %collective-permute-done.1 = bf16[64,2048]{1,0:T(8,128)(2,1)S(1)} collective-permute-done((bf16[64,2048]{1,0:T(8,128)(2,1)S(1)}, bf16[64,2048]{1,0:T(8,128)(2,1)S(1)}, u32[]{:S(2)}, u32[]{:S(2)}) %collective-permute-start.1) | collective-permute-done | bytes 262176 | tf_op jit(solution)/shard_map/ppermute | solution.py:53
  30.5 0.0 copy-done
  30.5 0.0 copy-start.1
  30.5 2.2 %collective-permute-start.2 = (bf16[128,2048]{1,0:T(8,128)(2,1)S(1)}, bf16[128,2048]{1,0:T(8,128)(2,1)S(1)}, u32[]{:S(2)}, u32[]{:S(2)}) collective-permute-start(bf16[128,2048]{1,0:T(8,128)(2,1)S(1)} %pad_maximum_fusion.1), channel_id=1, source_target_pairs={{0,96},{32,64},{64,32},{96,0},{16,48},{48,16},{80,112},{112,80},{1... | collective-permute-start | bytes 1572872 | tf_op jit(solution)/shard_map/ppermute | solution.py:53
  32.8 2.5 %collective-permute-done.6 = bf16[128,2048]{1,0:T(8,128)(2,1)S(1)} collective-permute-done((bf16[128,2048]{1,0:T(8,128)(2,1)S(1)}, bf16[128,2048]{1,0:T(8,128)(2,1)S(1)}, u32[]{:S(2)}, u32[]{:S(2)}) %collective-permute-start.6) | collective-permute-done | bytes 524320 | tf_op jit(solution)/shard_map/ppermute | solution.py:53
  35.4 1.9 %collective-permute-start.8 = (bf16[256,2048]{1,0:T(8,128)(2,1)S(1)}, bf16[256,2048]{1,0:T(8,128)(2,1)S(1)}, u32[]{:S(2)}, u32[]{:S(2)}) collective-permute-start(bf16[256,2048]{1,0:T(8,128)(2,1)S(1)} %constant_dynamic-update-slice_fusion), channel_id=1, source_target_pairs={{0,16},{16,0},{1,17},{17,1},{2,18},{18,2},{3,19},{19,3},{4,20},{20... | collective-permute-start | bytes 3145736 | tf_op jit(solution)/shard_map/ppermute | solution.py:76
  37.3 4.6 %collective-permute-done.2 = bf16[128,2048]{1,0:T(8,128)(2,1)S(1)} collective-permute-done((bf16[128,2048]{1,0:T(8,128)(2,1)S(1)}, bf16[128,2048]{1,0:T(8,128)(2,1)S(1)}, u32[]{:S(2)}, u32[]{:S(2)}) %collective-permute-start.2) | collective-permute-done | bytes 524320 | tf_op jit(solution)/shard_map/ppermute | solution.py:53
  41.9 0.1 pad_maximum_fusion
  42.0 1.9 %collective-permute-start.7 = (bf16[256,2048]{1,0:T(8,128)(2,1)S(1)}, bf16[256,2048]{1,0:T(8,128)(2,1)S(1)}, u32[]{:S(2)}, u32[]{:S(2)}) collective-permute-start(bf16[256,2048]{1,0:T(8,128)(2,1)S(1)} %pad_maximum_fusion), channel_id=1, source_target_pairs={{0,16},{16,0},{1,17},{17,1},{2,18},{18,2},{3,19},{19,3},{4,20},{20... | collective-permute-start | bytes 3145736 | tf_op jit(solution)/shard_map/ppermute | solution.py:76
  43.9 0.0 copy-done.1
  43.9 1.3 %convolution_convert_fusion.2 = bf16[256,1024]{1,0:T(8,128)(2,1)S(1)} fusion(bf16[256,2048]{1,0:T(8,128)(2,1)S(1)} %constant_dynamic-update-slice_fusion, bf16[1024,2048]{1,0:T(8,128)(2,1)S(1)} %copy-done.1), kind=kOutput, calls=%fused_computation.2 | convolution fusion | flops 1074003968 | bytes 5767168 | tf_op jit(solution)/shard_map/dot_general | solution.py:36
  45.2 1.3 %convolution_convert_fusion.3 = bf16[256,1024]{1,0:T(8,128)(2,1)S(1)} fusion(bf16[1024,2048]{1,0:T(8,128)(2,1)S(1)} %copy-done.1, bf16[128,2048]{1,0:T(8,128)(2,1)S(1)} %collective-permute-done.2, bf16[64,2048]{1,0:T(8,128)(2,1)S(1)} %collective-permute-done.1, bf16[32,2048]{1,0:T(8,128)(2,1)S(1)} %collective-permute-done, bf16[32,2048]{1,0:T(8,128)(2,1)S(1)} %copy-done), kind=kOutput, calls=%fused_computation.3 | convolution fusion | flops 1078198272 | bytes 5767168 | tf_op jit(solution)/shard_map/dot_general | solution.py:36
  46.5 0.2 select_bitcast_fusion.31
  46.7 0.0 collective-permute-done.8
  46.8 1.3 %convolution_convert_fusion = bf16[256,1024]{1,0:T(8,128)(2,1)S(1)} fusion(bf16[256,2048]{1,0:T(8,128)(2,1)S(1)} %collective-permute-done.8, bf16[1024,2048]{1,0:T(8,128)(2,1)S(1)} %copy-done.1), kind=kOutput, calls=%fused_computation | convolution fusion | flops 1074003968 | bytes 5767168 | tf_op jit(solution)/shard_map/dot_general | solution.py:36
  48.0 0.0 collective-permute-done.7
  48.1 1.3 %convolution_convert_fusion.1 = bf16[256,1024]{1,0:T(8,128)(2,1)S(1)} fusion(bf16[256,2048]{1,0:T(8,128)(2,1)S(1)} %collective-permute-done.7, bf16[1024,2048]{1,0:T(8,128)(2,1)S(1)} %copy-done.1), kind=kOutput, calls=%fused_computation.1 | convolution fusion | flops 1074003968 | bytes 5767168 | tf_op jit(solution)/shard_map/dot_general | solution.py:36
  49.3 0.2 select_bitcast_fusion.30
  49.7 0.1 pad_maximum_fusion.4
  49.8 2.2 %collective-permute-start.11 = (bf16[2,2,64,1024]{3,2,1,0:T(8,128)(2,1)S(1)}, bf16[2,2,64,1024]{3,2,1,0:T(8,128)(2,1)S(1)}, u32[]{:S(2)}, u32[]{:S(2)}) collective-permute-start(bf16[2,2,64,1024]{3,2,1,0:T(8,128)(2,1)S(1)} %pad_maximum_fusion.4), channel_id=1, source_target_pairs={{0,4},{4,0},{8,12},{12,8},{16,28},{20,24},{24,20},{28,16},{1,5},{5... | collective-permute-start | bytes 1572872 | tf_op jit(solution)/shard_map/ppermute | solution.py:53
  52.1 0.1 pad_maximum_fusion.3
  52.2 3.6 %collective-permute-start.9 = (bf16[2,2,64,1024]{3,2,1,0:T(8,128)(2,1)S(1)}, bf16[2,2,64,1024]{3,2,1,0:T(8,128)(2,1)S(1)}, u32[]{:S(2)}, u32[]{:S(2)}) collective-permute-start(bf16[2,2,64,1024]{3,2,1,0:T(8,128)(2,1)S(1)} %pad_maximum_fusion.3), channel_id=1, source_target_pairs={{0,4},{4,0},{8,12},{12,8},{16,28},{20,24},{24,20},{28,16},{1,5},{5... | collective-permute-start | bytes 1572872 | tf_op jit(solution)/shard_map/ppermute | solution.py:53
  55.9 5.0 %collective-permute-done.11 = bf16[2,2,64,1024]{3,2,1,0:T(8,128)(2,1)S(1)} collective-permute-done((bf16[2,2,64,1024]{3,2,1,0:T(8,128)(2,1)S(1)}, bf16[2,2,64,1024]{3,2,1,0:T(8,128)(2,1)S(1)}, u32[]{:S(2)}, u32[]{:S(2)}) %collective-permute-start.11) | collective-permute-done | bytes 524320 | tf_op jit(solution)/shard_map/ppermute | solution.py:53
  60.8 0.1 convert_element_type.68
  61.0 0.1 fusion.1
  61.0 3.5 %collective-permute-start.12 = (bf16[2,64,1024]{2,1,0:T(8,128)(2,1)S(1)}, bf16[2,64,1024]{2,1,0:T(8,128)(2,1)S(1)}, u32[]{:S(2)}, u32[]{:S(2)}) collective-permute-start(bf16[2,64,1024]{2,1,0:T(8,128)(2,1)S(1)} %fusion.1), channel_id=1, source_target_pairs={{0,12},{4,8},{8,4},{12,0},{16,20},{20,16},{24,28},{28,24},{1,13},{... | collective-permute-start | bytes 786440 | tf_op jit(solution)/shard_map/ppermute | solution.py:53
  64.6 2.2 %collective-permute-done.9 = bf16[2,2,64,1024]{3,2,1,0:T(8,128)(2,1)S(1)} collective-permute-done((bf16[2,2,64,1024]{3,2,1,0:T(8,128)(2,1)S(1)}, bf16[2,2,64,1024]{3,2,1,0:T(8,128)(2,1)S(1)}, u32[]{:S(2)}, u32[]{:S(2)}) %collective-permute-start.9) | collective-permute-done | bytes 524320 | tf_op jit(solution)/shard_map/ppermute | solution.py:53
  66.8 0.1 convert_element_type.63
  66.9 0.1 fusion.6
  67.0 3.5 %collective-permute-start.10 = (bf16[2,64,1024]{2,1,0:T(8,128)(2,1)S(1)}, bf16[2,64,1024]{2,1,0:T(8,128)(2,1)S(1)}, u32[]{:S(2)}, u32[]{:S(2)}) collective-permute-start(bf16[2,64,1024]{2,1,0:T(8,128)(2,1)S(1)} %fusion.6), channel_id=1, source_target_pairs={{0,12},{4,8},{8,4},{12,0},{16,20},{20,16},{24,28},{28,24},{1,13},{... | collective-permute-start | bytes 786440 | tf_op jit(solution)/shard_map/ppermute | solution.py:53
  70.5 0.0 collective-permute-done.12
  70.5 0.1 fusion.4
  70.6 9.1 %collective-permute-start.13 = (bf16[2,64,1024]{2,1,0:T(8,128)(2,1)S(1)}, bf16[2,64,1024]{2,1,0:T(8,128)(2,1)S(1)}, u32[]{:S(2)}, u32[]{:S(2)}) collective-permute-start(bf16[2,64,1024]{2,1,0:T(8,128)(2,1)S(1)} %fusion.4), channel_id=1, source_target_pairs={{0,1},{1,0},{2,3},{3,2},{16,19},{17,18},{18,17},{19,16},{4,5},{5,4... | collective-permute-start | bytes 786440 | tf_op jit(solution)/shard_map/ppermute | solution.py:53
  79.7 0.0 collective-permute-done.10
  79.7 12.5 %collective-permute-done.13 = bf16[2,64,1024]{2,1,0:T(8,128)(2,1)S(1)} collective-permute-done((bf16[2,64,1024]{2,1,0:T(8,128)(2,1)S(1)}, bf16[2,64,1024]{2,1,0:T(8,128)(2,1)S(1)}, u32[]{:S(2)}, u32[]{:S(2)}) %collective-permute-start.13) | collective-permute-done | bytes 262176 | tf_op jit(solution)/shard_map/ppermute | solution.py:53
  92.3 0.1 fusion.9
  92.4 12.2 %collective-permute-start.14 = (bf16[64,1024]{1,0:T(8,128)(2,1)S(1)}, bf16[64,1024]{1,0:T(8,128)(2,1)S(1)}, u32[]{:S(2)}, u32[]{:S(2)}) collective-permute-start(bf16[64,1024]{1,0:T(8,128)(2,1)S(1)} %fusion.12), channel_id=1, source_target_pairs={{0,3},{1,2},{2,1},{3,0},{16,17},{17,16},{18,19},{19,18},{4,7},{5,6... | collective-permute-start | bytes 393224 | tf_op jit(solution)/shard_map/ppermute | solution.py:53
  104.6 5.2 %collective-permute-done.14 = bf16[64,1024]{1,0:T(8,128)(2,1)S(1)} collective-permute-done((bf16[64,1024]{1,0:T(8,128)(2,1)S(1)}, bf16[64,1024]{1,0:T(8,128)(2,1)S(1)}, u32[]{:S(2)}, u32[]{:S(2)}) %collective-permute-start.14) | collective-permute-done | bytes 131104 | tf_op jit(solution)/shard_map/ppermute | solution.py:53
  109.9 0.7 reverse_select_fusion
  (21 shorter events, 0.5 us)
Async XLA Ops:
  2.0 28.5 %copy-start = (bf16[32,2048]{1,0:T(8,128)(2,1)S(1)}, bf16[32,2048]{1,0:T(8,128)(2,1)}, u32[]{:S(2)}) copy-start(bf16[32,2048]{1,0:T(8,128)(2,1)} %shard_map.37) | copy-start | bytes 393220
  2.0 13.7 %collective-permute-start.3 = (bf16[32,2048]{1,0:T(8,128)(2,1)}, bf16[32,2048]{1,0:T(8,128)(2,1)S(1)}, u32[]{:S(2)}, u32[]{:S(2)}) collective-permute-start(bf16[32,2048]{1,0:T(8,128)(2,1)} %shard_map.37), channel_id=1, source_target_pairs={{0,256},{128,384},{256,0},{384,128},{1,257},{129,385},{257,1},{385... | collective-permute-start | bytes 393224 | tf_op jit(solution)/shard_map/ppermute | solution.py:32
  7.3 8.4 %collective-permute-start.4 = (bf16[32,2048]{1,0:T(8,128)(2,1)}, bf16[32,2048]{1,0:T(8,128)(2,1)S(1)}, u32[]{:S(2)}, u32[]{:S(2)}) collective-permute-start(bf16[32,2048]{1,0:T(8,128)(2,1)} %shard_map.37), channel_id=1, source_target_pairs={{0,384},{128,0},{256,128},{384,256},{1,385},{129,1},{257,129},{385... | collective-permute-start | bytes 393224 | tf_op jit(solution)/shard_map/ppermute | solution.py:32
  9.4 10.5 %collective-permute-start = (bf16[32,2048]{1,0:T(8,128)(2,1)}, bf16[32,2048]{1,0:T(8,128)(2,1)S(1)}, u32[]{:S(2)}, u32[]{:S(2)}) collective-permute-start(bf16[32,2048]{1,0:T(8,128)(2,1)} %shard_map.37), channel_id=1, source_target_pairs={{0,128},{128,256},{256,384},{384,0},{1,129},{129,257},{257,385},{3... | collective-permute-start | bytes 393224 | tf_op jit(solution)/shard_map/ppermute | solution.py:32
  15.7 8.5 %collective-permute-start.5 = (bf16[64,2048]{1,0:T(8,128)(2,1)S(1)}, bf16[64,2048]{1,0:T(8,128)(2,1)S(1)}, u32[]{:S(2)}, u32[]{:S(2)}) collective-permute-start(bf16[64,2048]{1,0:T(8,128)(2,1)S(1)} %pad_maximum_fusion.6), channel_id=1, source_target_pairs={{0,32},{32,0},{64,96},{96,64},{16,112},{48,80},{80,48},{112,16},{1... | collective-permute-start | bytes 786440 | tf_op jit(solution)/shard_map/ppermute | solution.py:53
  20.8 9.7 %collective-permute-start.1 = (bf16[64,2048]{1,0:T(8,128)(2,1)S(1)}, bf16[64,2048]{1,0:T(8,128)(2,1)S(1)}, u32[]{:S(2)}, u32[]{:S(2)}) collective-permute-start(bf16[64,2048]{1,0:T(8,128)(2,1)S(1)} %pad_maximum_fusion.5), channel_id=1, source_target_pairs={{0,32},{32,0},{64,96},{96,64},{16,112},{48,80},{80,48},{112,16},{1... | collective-permute-start | bytes 786440 | tf_op jit(solution)/shard_map/ppermute | solution.py:53
  24.2 11.1 %collective-permute-start.6 = (bf16[128,2048]{1,0:T(8,128)(2,1)S(1)}, bf16[128,2048]{1,0:T(8,128)(2,1)S(1)}, u32[]{:S(2)}, u32[]{:S(2)}) collective-permute-start(bf16[128,2048]{1,0:T(8,128)(2,1)S(1)} %pad_maximum_fusion.2), channel_id=1, source_target_pairs={{0,96},{32,64},{64,32},{96,0},{16,48},{48,16},{80,112},{112,80},{1... | collective-permute-start | bytes 1572872 | tf_op jit(solution)/shard_map/ppermute | solution.py:53
  30.5 13.4 %copy-start.1 = (bf16[1024,2048]{1,0:T(8,128)(2,1)S(1)}, bf16[1024,2048]{1,0:T(8,128)(2,1)}, u32[]{:S(2)}) copy-start(bf16[1024,2048]{1,0:T(8,128)(2,1)} %param.3) | copy-start | bytes 12582916
  30.5 11.3 %collective-permute-start.2 = (bf16[128,2048]{1,0:T(8,128)(2,1)S(1)}, bf16[128,2048]{1,0:T(8,128)(2,1)S(1)}, u32[]{:S(2)}, u32[]{:S(2)}) collective-permute-start(bf16[128,2048]{1,0:T(8,128)(2,1)S(1)} %pad_maximum_fusion.1), channel_id=1, source_target_pairs={{0,96},{32,64},{64,32},{96,0},{16,48},{48,16},{80,112},{112,80},{1... | collective-permute-start | bytes 1572872 | tf_op jit(solution)/shard_map/ppermute | solution.py:53
  35.4 11.4 %collective-permute-start.8 = (bf16[256,2048]{1,0:T(8,128)(2,1)S(1)}, bf16[256,2048]{1,0:T(8,128)(2,1)S(1)}, u32[]{:S(2)}, u32[]{:S(2)}) collective-permute-start(bf16[256,2048]{1,0:T(8,128)(2,1)S(1)} %constant_dynamic-update-slice_fusion), channel_id=1, source_target_pairs={{0,16},{16,0},{1,17},{17,1},{2,18},{18,2},{3,19},{19,3},{4,20},{20... | collective-permute-start | bytes 3145736 | tf_op jit(solution)/shard_map/ppermute | solution.py:76
  42.0 6.1 %collective-permute-start.7 = (bf16[256,2048]{1,0:T(8,128)(2,1)S(1)}, bf16[256,2048]{1,0:T(8,128)(2,1)S(1)}, u32[]{:S(2)}, u32[]{:S(2)}) collective-permute-start(bf16[256,2048]{1,0:T(8,128)(2,1)S(1)} %pad_maximum_fusion), channel_id=1, source_target_pairs={{0,16},{16,0},{1,17},{17,1},{2,18},{18,2},{3,19},{19,3},{4,20},{20... | collective-permute-start | bytes 3145736 | tf_op jit(solution)/shard_map/ppermute | solution.py:76
  49.8 11.1 %collective-permute-start.11 = (bf16[2,2,64,1024]{3,2,1,0:T(8,128)(2,1)S(1)}, bf16[2,2,64,1024]{3,2,1,0:T(8,128)(2,1)S(1)}, u32[]{:S(2)}, u32[]{:S(2)}) collective-permute-start(bf16[2,2,64,1024]{3,2,1,0:T(8,128)(2,1)S(1)} %pad_maximum_fusion.4), channel_id=1, source_target_pairs={{0,4},{4,0},{8,12},{12,8},{16,28},{20,24},{24,20},{28,16},{1,5},{5... | collective-permute-start | bytes 1572872 | tf_op jit(solution)/shard_map/ppermute | solution.py:53
  52.2 14.6 %collective-permute-start.9 = (bf16[2,2,64,1024]{3,2,1,0:T(8,128)(2,1)S(1)}, bf16[2,2,64,1024]{3,2,1,0:T(8,128)(2,1)S(1)}, u32[]{:S(2)}, u32[]{:S(2)}) collective-permute-start(bf16[2,2,64,1024]{3,2,1,0:T(8,128)(2,1)S(1)} %pad_maximum_fusion.3), channel_id=1, source_target_pairs={{0,4},{4,0},{8,12},{12,8},{16,28},{20,24},{24,20},{28,16},{1,5},{5... | collective-permute-start | bytes 1572872 | tf_op jit(solution)/shard_map/ppermute | solution.py:53
  61.0 9.5 %collective-permute-start.12 = (bf16[2,64,1024]{2,1,0:T(8,128)(2,1)S(1)}, bf16[2,64,1024]{2,1,0:T(8,128)(2,1)S(1)}, u32[]{:S(2)}, u32[]{:S(2)}) collective-permute-start(bf16[2,64,1024]{2,1,0:T(8,128)(2,1)S(1)} %fusion.1), channel_id=1, source_target_pairs={{0,12},{4,8},{8,4},{12,0},{16,20},{20,16},{24,28},{28,24},{1,13},{... | collective-permute-start | bytes 786440 | tf_op jit(solution)/shard_map/ppermute | solution.py:53
  67.0 12.7 %collective-permute-start.10 = (bf16[2,64,1024]{2,1,0:T(8,128)(2,1)S(1)}, bf16[2,64,1024]{2,1,0:T(8,128)(2,1)S(1)}, u32[]{:S(2)}, u32[]{:S(2)}) collective-permute-start(bf16[2,64,1024]{2,1,0:T(8,128)(2,1)S(1)} %fusion.6), channel_id=1, source_target_pairs={{0,12},{4,8},{8,4},{12,0},{16,20},{20,16},{24,28},{28,24},{1,13},{... | collective-permute-start | bytes 786440 | tf_op jit(solution)/shard_map/ppermute | solution.py:53
  70.6 21.7 %collective-permute-start.13 = (bf16[2,64,1024]{2,1,0:T(8,128)(2,1)S(1)}, bf16[2,64,1024]{2,1,0:T(8,128)(2,1)S(1)}, u32[]{:S(2)}, u32[]{:S(2)}) collective-permute-start(bf16[2,64,1024]{2,1,0:T(8,128)(2,1)S(1)} %fusion.4), channel_id=1, source_target_pairs={{0,1},{1,0},{2,3},{3,2},{16,19},{17,18},{18,17},{19,16},{4,5},{5,4... | collective-permute-start | bytes 786440 | tf_op jit(solution)/shard_map/ppermute | solution.py:53
  92.4 17.4 %collective-permute-start.14 = (bf16[64,1024]{1,0:T(8,128)(2,1)S(1)}, bf16[64,1024]{1,0:T(8,128)(2,1)S(1)}, u32[]{:S(2)}, u32[]{:S(2)}) collective-permute-start(bf16[64,1024]{1,0:T(8,128)(2,1)S(1)} %fusion.12), channel_id=1, source_target_pairs={{0,3},{1,2},{2,1},{3,0},{16,17},{17,16},{18,19},{19,18},{4,7},{5,6... | collective-permute-start | bytes 393224 | tf_op jit(solution)/shard_map/ppermute | solution.py:53

commit v4 on v3

--- a/solution.py
+++ b/solution.py
@@ -105,9 +105,11 @@
 
     far = sum_x([zh + step_zh, zh + 2])
     near = sum_x([zh, zh - step_zh])
-    near = near + halve(far.astype(jnp.bfloat16), "zh", True).astype(jnp.float32)
-    last = halve(near[1].astype(jnp.bfloat16), "zh", False).astype(jnp.float32)
-    scores = (near[0] + last).astype(jnp.bfloat16).reshape(2, count, width)
+    far = far.astype(jnp.bfloat16)
+    back = near[1] + halve(far[1], "zh", True).astype(jnp.float32)
+    last = halve(back.astype(jnp.bfloat16), "zh", False).astype(jnp.float32)
+    ahead = halve(far[0], "zh", True).astype(jnp.float32)
+    scores = (near[0] + ahead + last).astype(jnp.bfloat16).reshape(2, count, width)
     scores = jnp.where(core == 0, scores, scores[::-1])
     return scores.reshape(2 * count, width)
 

time: 111 us -> 105 us (0.946)
  the two profiles are of different devices: /device:TPU:40 before, /device:TPU:35 now
where the time goes in v4:
time: 105 us
  starting transfers between devices  63.9 us (61%)
  waiting for transfers between devices  29.6 us (28%)
  matrix products  5.12 us (5%)
  other arithmetic  3.23 us (3%)
  Pallas kernels  2.02 us (2%)
    ppermute x11, starting transfers between devices, halve(): return lax.ppermute(array, names, pairs)  44.9 us
    ppermute x11, waiting for transfers between devices, halve(): return lax.ppermute(array, names, pairs)  26.6 us
    ppermute x3, starting transfers between devices, shift(): lax.ppermute(array, axis, [(i, (i + step) % size) for i in range(size)])  10.3 us
    ppermute x2, starting transfers between devices, partials(): both = [rows, lax.ppermute(rows, 'core', [(0, 1), (1, 0)])]  8.7 us
    dot_general x4, matrix products, dot_t(): lax.dot_general(rows, train, (((1,), (1,)), ((), ())), preferred_element_...  5.12 us
    ppermute x3, waiting for transfers between devices, shift(): lax.ppermute(array, axis, [(i, (i + step) % size) for i in range(size)])  3.06 us
  transfers between devices with their start and end apart: 16, of which 9 were waited for; matrix products, arithmetic and copies ran while one was open for 6% of the time, Pallas kernels for 0%

profile of v4, /device:TPU:35, one launch (start us, length us, event | category | flops | bytes accessed | tf_op | source)
XLA Modules:
  0.0 104.8 jit_solution(372300407549389654)
XLA Ops:
  0.0 2.0 %shard_map.37 = bf16[32,2048]{1,0:T(8,128)(2,1)} custom-call(bf16[32,2048]{1,0:T(8,128)(2,1)} %rows_ref.1, bf16[16,128,128]{2,1,0:T(8,128)(2,1)} %precond_ref.1), custom_call_target="tpu_custom_call" | custom-call | tf_op jit(solution)/shard_map/pallas_call | solution.py:22
  2.0 0.0 copy-start
  2.0 5.0 %collective-permute-start.3 = (bf16[32,2048]{1,0:T(8,128)(2,1)}, bf16[32,2048]{1,0:T(8,128)(2,1)S(1)}, u32[]{:S(2)}, u32[]{:S(2)}) collective-permute-start(bf16[32,2048]{1,0:T(8,128)(2,1)} %shard_map.37), channel_id=1, source_target_pairs={{0,256},{128,384},{256,0},{384,128},{1,257},{129,385},{257,1},{385... | collective-permute-start | bytes 393224 | tf_op jit(solution)/shard_map/ppermute | solution.py:32
  7.1 1.9 %collective-permute-start.4 = (bf16[32,2048]{1,0:T(8,128)(2,1)}, bf16[32,2048]{1,0:T(8,128)(2,1)S(1)}, u32[]{:S(2)}, u32[]{:S(2)}) collective-permute-start(bf16[32,2048]{1,0:T(8,128)(2,1)} %shard_map.37), channel_id=1, source_target_pairs={{0,384},{128,0},{256,128},{384,256},{1,385},{129,1},{257,129},{385... | collective-permute-start | bytes 393224 | tf_op jit(solution)/shard_map/ppermute | solution.py:32
  9.0 3.4 %collective-permute-start = (bf16[32,2048]{1,0:T(8,128)(2,1)}, bf16[32,2048]{1,0:T(8,128)(2,1)S(1)}, u32[]{:S(2)}, u32[]{:S(2)}) collective-permute-start(bf16[32,2048]{1,0:T(8,128)(2,1)} %shard_map.37), channel_id=1, source_target_pairs={{0,128},{128,256},{256,384},{384,0},{1,129},{129,257},{257,385},{3... | collective-permute-start | bytes 393224 | tf_op jit(solution)/shard_map/ppermute | solution.py:32
  12.7 3.1 %collective-permute-done.3 = bf16[32,2048]{1,0:T(8,128)(2,1)S(1)} collective-permute-done((bf16[32,2048]{1,0:T(8,128)(2,1)}, bf16[32,2048]{1,0:T(8,128)(2,1)S(1)}, u32[]{:S(2)}, u32[]{:S(2)}) %collective-permute-start.3) | collective-permute-done | bytes 131104 | tf_op jit(solution)/shard_map/ppermute | solution.py:32
  15.8 0.0 collective-permute-done.4
  15.8 4.6 %collective-permute-start.5 = (bf16[64,2048]{1,0:T(8,128)(2,1)S(1)}, bf16[64,2048]{1,0:T(8,128)(2,1)S(1)}, u32[]{:S(2)}, u32[]{:S(2)}) collective-permute-start(bf16[64,2048]{1,0:T(8,128)(2,1)S(1)} %pad_maximum_fusion.6), channel_id=1, source_target_pairs={{0,32},{32,0},{64,96},{96,64},{16,112},{48,80},{80,48},{112,16},{1... | collective-permute-start | bytes 786440 | tf_op jit(solution)/shard_map/ppermute | solution.py:53
  20.4 0.0 collective-permute-done
  20.5 0.9 pad_maximum_fusion.5
  21.4 2.8 %collective-permute-start.1 = (bf16[64,2048]{1,0:T(8,128)(2,1)S(1)}, bf16[64,2048]{1,0:T(8,128)(2,1)S(1)}, u32[]{:S(2)}, u32[]{:S(2)}) collective-permute-start(bf16[64,2048]{1,0:T(8,128)(2,1)S(1)} %pad_maximum_fusion.5), channel_id=1, source_target_pairs={{0,32},{32,0},{64,96},{96,64},{16,112},{48,80},{80,48},{112,16},{1... | collective-permute-start | bytes 786440 | tf_op jit(solution)/shard_map/ppermute | solution.py:53
  24.2 0.0 collective-permute-done.5
  24.2 2.2 %collective-permute-start.6 = (bf16[128,2048]{1,0:T(8,128)(2,1)S(1)}, bf16[128,2048]{1,0:T(8,128)(2,1)S(1)}, u32[]{:S(2)}, u32[]{:S(2)}) collective-permute-start(bf16[128,2048]{1,0:T(8,128)(2,1)S(1)} %pad_maximum_fusion.2), channel_id=1, source_target_pairs={{0,96},{32,64},{64,32},{96,0},{16,48},{48,16},{80,112},{112,80},{1... | collective-permute-start | bytes 1572872 | tf_op jit(solution)/shard_map/ppermute | solution.py:53
  26.5 3.2 %collective-permute-done.1 = bf16[64,2048]{1,0:T(8,128)(2,1)S(1)} collective-permute-done((bf16[64,2048]{1,0:T(8,128)(2,1)S(1)}, bf16[64,2048]{1,0:T(8,128)(2,1)S(1)}, u32[]{:S(2)}, u32[]{:S(2)}) %collective-permute-start.1) | collective-permute-done | bytes 262176 | tf_op jit(solution)/shard_map/ppermute | solution.py:53
  29.7 0.0 copy-done
  29.7 0.0 copy-start.1
  29.8 2.2 %collective-permute-start.2 = (bf16[128,2048]{1,0:T(8,128)(2,1)S(1)}, bf16[128,2048]{1,0:T(8,128)(2,1)S(1)}, u32[]{:S(2)}, u32[]{:S(2)}) collective-permute-start(bf16[128,2048]{1,0:T(8,128)(2,1)S(1)} %pad_maximum_fusion.1), channel_id=1, source_target_pairs={{0,96},{32,64},{64,32},{96,0},{16,48},{48,16},{80,112},{112,80},{1... | collective-permute-start | bytes 1572872 | tf_op jit(solution)/shard_map/ppermute | solution.py:53
  32.0 2.5 %collective-permute-done.6 = bf16[128,2048]{1,0:T(8,128)(2,1)S(1)} collective-permute-done((bf16[128,2048]{1,0:T(8,128)(2,1)S(1)}, bf16[128,2048]{1,0:T(8,128)(2,1)S(1)}, u32[]{:S(2)}, u32[]{:S(2)}) %collective-permute-start.6) | collective-permute-done | bytes 524320 | tf_op jit(solution)/shard_map/ppermute | solution.py:53
  34.5 4.4 %collective-permute-start.8 = (bf16[256,2048]{1,0:T(8,128)(2,1)S(1)}, bf16[256,2048]{1,0:T(8,128)(2,1)S(1)}, u32[]{:S(2)}, u32[]{:S(2)}) collective-permute-start(bf16[256,2048]{1,0:T(8,128)(2,1)S(1)} %constant_dynamic-update-slice_fusion), channel_id=1, source_target_pairs={{0,16},{16,0},{1,17},{17,1},{2,18},{18,2},{3,19},{19,3},{4,20},{20... | collective-permute-start | bytes 3145736 | tf_op jit(solution)/shard_map/ppermute | solution.py:76
  38.9 1.3 %collective-permute-done.2 = bf16[128,2048]{1,0:T(8,128)(2,1)S(1)} collective-permute-done((bf16[128,2048]{1,0:T(8,128)(2,1)S(1)}, bf16[128,2048]{1,0:T(8,128)(2,1)S(1)}, u32[]{:S(2)}, u32[]{:S(2)}) %collective-permute-start.2) | collective-permute-done | bytes 524320 | tf_op jit(solution)/shard_map/ppermute | solution.py:53
  40.2 0.1 pad_maximum_fusion
  40.3 4.3 %collective-permute-start.7 = (bf16[256,2048]{1,0:T(8,128)(2,1)S(1)}, bf16[256,2048]{1,0:T(8,128)(2,1)S(1)}, u32[]{:S(2)}, u32[]{:S(2)}) collective-permute-start(bf16[256,2048]{1,0:T(8,128)(2,1)S(1)} %pad_maximum_fusion), channel_id=1, source_target_pairs={{0,16},{16,0},{1,17},{17,1},{2,18},{18,2},{3,19},{19,3},{4,20},{20... | collective-permute-start | bytes 3145736 | tf_op jit(solution)/shard_map/ppermute | solution.py:76
  44.6 0.0 copy-done.1
  44.6 1.3 %convolution_convert_fusion.2 = bf16[256,1024]{1,0:T(8,128)(2,1)S(1)} fusion(bf16[256,2048]{1,0:T(8,128)(2,1)S(1)} %constant_dynamic-update-slice_fusion, bf16[1024,2048]{1,0:T(8,128)(2,1)S(1)} %copy-done.1), kind=kOutput, calls=%fused_computation.2 | convolution fusion | flops 1074003968 | bytes 5767168 | tf_op jit(solution)/shard_map/dot_general | solution.py:36
  45.9 1.3 %convolution_convert_fusion.3 = bf16[256,1024]{1,0:T(8,128)(2,1)S(1)} fusion(bf16[1024,2048]{1,0:T(8,128)(2,1)S(1)} %copy-done.1, bf16[128,2048]{1,0:T(8,128)(2,1)S(1)} %collective-permute-done.2, bf16[64,2048]{1,0:T(8,128)(2,1)S(1)} %collective-permute-done.1, bf16[32,2048]{1,0:T(8,128)(2,1)S(1)} %collective-permute-done, bf16[32,2048]{1,0:T(8,128)(2,1)S(1)} %copy-done), kind=kOutput, calls=%fused_computation.3 | convolution fusion | flops 1078198272 | bytes 5767168 | tf_op jit(solution)/shard_map/dot_general | solution.py:36
  47.2 0.2 select_bitcast_fusion.15
  47.5 0.0 collective-permute-done.8
  47.5 1.3 %convolution_convert_fusion = bf16[256,1024]{1,0:T(8,128)(2,1)S(1)} fusion(bf16[256,2048]{1,0:T(8,128)(2,1)S(1)} %collective-permute-done.8, bf16[1024,2048]{1,0:T(8,128)(2,1)S(1)} %copy-done.1), kind=kOutput, calls=%fused_computation | convolution fusion | flops 1074003968 | bytes 5767168 | tf_op jit(solution)/shard_map/dot_general | solution.py:36
  48.8 0.0 collective-permute-done.7
  48.8 1.3 %convolution_convert_fusion.1 = bf16[256,1024]{1,0:T(8,128)(2,1)S(1)} fusion(bf16[256,2048]{1,0:T(8,128)(2,1)S(1)} %collective-permute-done.7, bf16[1024,2048]{1,0:T(8,128)(2,1)S(1)} %copy-done.1), kind=kOutput, calls=%fused_computation.1 | convolution fusion | flops 1074003968 | bytes 5767168 | tf_op jit(solution)/shard_map/dot_general | solution.py:36
  50.1 0.2 select_bitcast_fusion.14
  50.4 0.1 pad_maximum_fusion.4
  50.5 3.1 %collective-permute-start.11 = (bf16[2,2,64,1024]{3,2,1,0:T(8,128)(2,1)S(1)}, bf16[2,2,64,1024]{3,2,1,0:T(8,128)(2,1)S(1)}, u32[]{:S(2)}, u32[]{:S(2)}) collective-permute-start(bf16[2,2,64,1024]{3,2,1,0:T(8,128)(2,1)S(1)} %pad_maximum_fusion.4), channel_id=1, source_target_pairs={{0,4},{4,0},{8,12},{12,8},{16,28},{20,24},{24,20},{28,16},{1,5},{5... | collective-permute-start | bytes 1572872 | tf_op jit(solution)/shard_map/ppermute | solution.py:53
  53.7 0.1 pad_maximum_fusion.3
  53.8 2.2 %collective-permute-start.9 = (bf16[2,2,64,1024]{3,2,1,0:T(8,128)(2,1)S(1)}, bf16[2,2,64,1024]{3,2,1,0:T(8,128)(2,1)S(1)}, u32[]{:S(2)}, u32[]{:S(2)}) collective-permute-start(bf16[2,2,64,1024]{3,2,1,0:T(8,128)(2,1)S(1)} %pad_maximum_fusion.3), channel_id=1, source_target_pairs={{0,4},{4,0},{8,12},{12,8},{16,28},{20,24},{24,20},{28,16},{1,5},{5... | collective-permute-start | bytes 1572872 | tf_op jit(solution)/shard_map/ppermute | solution.py:53
  56.0 4.7 %collective-permute-done.11 = bf16[2,2,64,1024]{3,2,1,0:T(8,128)(2,1)S(1)} collective-permute-done((bf16[2,2,64,1024]{3,2,1,0:T(8,128)(2,1)S(1)}, bf16[2,2,64,1024]{3,2,1,0:T(8,128)(2,1)S(1)}, u32[]{:S(2)}, u32[]{:S(2)}) %collective-permute-start.11) | collective-permute-done | bytes 524320 | tf_op jit(solution)/shard_map/ppermute | solution.py:53
  60.7 0.1 convert_element_type.70
  60.8 0.1 fusion.1
  60.9 4.9 %collective-permute-start.12 = (bf16[2,64,1024]{2,1,0:T(8,128)(2,1)S(1)}, bf16[2,64,1024]{2,1,0:T(8,128)(2,1)S(1)}, u32[]{:S(2)}, u32[]{:S(2)}) collective-permute-start(bf16[2,64,1024]{2,1,0:T(8,128)(2,1)S(1)} %fusion.1), channel_id=1, source_target_pairs={{0,12},{4,8},{8,4},{12,0},{16,20},{20,16},{24,28},{28,24},{1,13},{... | collective-permute-start | bytes 786440 | tf_op jit(solution)/shard_map/ppermute | solution.py:53
  65.8 0.5 collective-permute-done.9
  66.3 0.1 convert_element_type.65
  66.4 0.1 fusion.6
  66.5 4.9 %collective-permute-start.10 = (bf16[2,64,1024]{2,1,0:T(8,128)(2,1)S(1)}, bf16[2,64,1024]{2,1,0:T(8,128)(2,1)S(1)}, u32[]{:S(2)}, u32[]{:S(2)}) collective-permute-start(bf16[2,64,1024]{2,1,0:T(8,128)(2,1)S(1)} %fusion.6), channel_id=1, source_target_pairs={{0,12},{4,8},{8,4},{12,0},{16,20},{20,16},{24,28},{28,24},{1,13},{... | collective-permute-start | bytes 786440 | tf_op jit(solution)/shard_map/ppermute | solution.py:53
  71.4 0.0 collective-permute-done.12
  71.4 0.1 fusion.4
  71.5 12.5 %collective-permute-start.14 = (bf16[64,1024]{1,0:T(8,128)(2,1)S(1)}, bf16[64,1024]{1,0:T(8,128)(2,1)S(1)}, u32[]{:S(2)}, u32[]{:S(2)}) collective-permute-start(bf16[64,1024]{1,0:T(8,128)(2,1)S(1)} %get-tuple-element.38), channel_id=1, source_target_pairs={{0,1},{1,0},{2,3},{3,2},{16,19},{17,18},{18,17},{19,16},{4,5},{5,4... | collective-permute-start | bytes 393224 | tf_op jit(solution)/shard_map/ppermute | solution.py:53
  84.0 1.9 %collective-permute-start.13 = (bf16[64,1024]{1,0:T(8,128)(2,1)S(1)}, bf16[64,1024]{1,0:T(8,128)(2,1)S(1)}, u32[]{:S(2)}, u32[]{:S(2)}) collective-permute-start(bf16[64,1024]{1,0:T(8,128)(2,1)S(1)} %get-tuple-element.37), channel_id=1, source_target_pairs={{0,1},{1,0},{2,3},{3,2},{16,19},{17,18},{18,17},{19,16},{4,5},{5,4... | collective-permute-start | bytes 393224 | tf_op jit(solution)/shard_map/ppermute | solution.py:53
  85.9 0.0 collective-permute-done.10
  86.0 0.1 fusion.8
  86.0 4.2 %collective-permute-done.14 = bf16[64,1024]{1,0:T(8,128)(2,1)S(1)} collective-permute-done((bf16[64,1024]{1,0:T(8,128)(2,1)S(1)}, bf16[64,1024]{1,0:T(8,128)(2,1)S(1)}, u32[]{:S(2)}, u32[]{:S(2)}) %collective-permute-start.14) | collective-permute-done | bytes 131104 | tf_op jit(solution)/shard_map/ppermute | solution.py:53
  90.3 3.7 %collective-permute-start.15 = (bf16[64,1024]{1,0:T(8,128)(2,1)S(1)}, bf16[64,1024]{1,0:T(8,128)(2,1)S(1)}, u32[]{:S(2)}, u32[]{:S(2)}) collective-permute-start(bf16[64,1024]{1,0:T(8,128)(2,1)S(1)} %fusion.10), channel_id=1, source_target_pairs={{0,3},{1,2},{2,1},{3,0},{16,17},{17,16},{18,19},{19,18},{4,7},{5,6... | collective-permute-start | bytes 393224 | tf_op jit(solution)/shard_map/ppermute | solution.py:53
  94.0 1.3 %collective-permute-done.13 = bf16[64,1024]{1,0:T(8,128)(2,1)S(1)} collective-permute-done((bf16[64,1024]{1,0:T(8,128)(2,1)S(1)}, bf16[64,1024]{1,0:T(8,128)(2,1)S(1)}, u32[]{:S(2)}, u32[]{:S(2)}) %collective-permute-start.13) | collective-permute-done | bytes 131104 | tf_op jit(solution)/shard_map/ppermute | solution.py:53
  95.3 8.8 %collective-permute-done.15 = bf16[64,1024]{1,0:T(8,128)(2,1)S(1)} collective-permute-done((bf16[64,1024]{1,0:T(8,128)(2,1)S(1)}, bf16[64,1024]{1,0:T(8,128)(2,1)S(1)}, u32[]{:S(2)}, u32[]{:S(2)}) %collective-permute-start.15) | collective-permute-done | bytes 131104 | tf_op jit(solution)/shard_map/ppermute | solution.py:53
  104.2 0.7 reverse_select_fusion
  (22 shorter events, 0.5 us)
Async XLA Ops:
  2.0 27.7 %copy-start = (bf16[32,2048]{1,0:T(8,128)(2,1)S(1)}, bf16[32,2048]{1,0:T(8,128)(2,1)}, u32[]{:S(2)}) copy-start(bf16[32,2048]{1,0:T(8,128)(2,1)} %shard_map.37) | copy-start | bytes 393220
  2.0 13.7 %collective-permute-start.3 = (bf16[32,2048]{1,0:T(8,128)(2,1)}, bf16[32,2048]{1,0:T(8,128)(2,1)S(1)}, u32[]{:S(2)}, u32[]{:S(2)}) collective-permute-start(bf16[32,2048]{1,0:T(8,128)(2,1)} %shard_map.37), channel_id=1, source_target_pairs={{0,256},{128,384},{256,0},{384,128},{1,257},{129,385},{257,1},{385... | collective-permute-start | bytes 393224 | tf_op jit(solution)/shard_map/ppermute | solution.py:32
  7.1 8.7 %collective-permute-start.4 = (bf16[32,2048]{1,0:T(8,128)(2,1)}, bf16[32,2048]{1,0:T(8,128)(2,1)S(1)}, u32[]{:S(2)}, u32[]{:S(2)}) collective-permute-start(bf16[32,2048]{1,0:T(8,128)(2,1)} %shard_map.37), channel_id=1, source_target_pairs={{0,384},{128,0},{256,128},{384,256},{1,385},{129,1},{257,129},{385... | collective-permute-start | bytes 393224 | tf_op jit(solution)/shard_map/ppermute | solution.py:32
  9.0 11.5 %collective-permute-start = (bf16[32,2048]{1,0:T(8,128)(2,1)}, bf16[32,2048]{1,0:T(8,128)(2,1)S(1)}, u32[]{:S(2)}, u32[]{:S(2)}) collective-permute-start(bf16[32,2048]{1,0:T(8,128)(2,1)} %shard_map.37), channel_id=1, source_target_pairs={{0,128},{128,256},{256,384},{384,0},{1,129},{129,257},{257,385},{3... | collective-permute-start | bytes 393224 | tf_op jit(solution)/shard_map/ppermute | solution.py:32
  15.8 8.4 %collective-permute-start.5 = (bf16[64,2048]{1,0:T(8,128)(2,1)S(1)}, bf16[64,2048]{1,0:T(8,128)(2,1)S(1)}, u32[]{:S(2)}, u32[]{:S(2)}) collective-permute-start(bf16[64,2048]{1,0:T(8,128)(2,1)S(1)} %pad_maximum_fusion.6), channel_id=1, source_target_pairs={{0,32},{32,0},{64,96},{96,64},{16,112},{48,80},{80,48},{112,16},{1... | collective-permute-start | bytes 786440 | tf_op jit(solution)/shard_map/ppermute | solution.py:53
  21.4 8.3 %collective-permute-start.1 = (bf16[64,2048]{1,0:T(8,128)(2,1)S(1)}, bf16[64,2048]{1,0:T(8,128)(2,1)S(1)}, u32[]{:S(2)}, u32[]{:S(2)}) collective-permute-start(bf16[64,2048]{1,0:T(8,128)(2,1)S(1)} %pad_maximum_fusion.5), channel_id=1, source_target_pairs={{0,32},{32,0},{64,96},{96,64},{16,112},{48,80},{80,48},{112,16},{1... | collective-permute-start | bytes 786440 | tf_op jit(solution)/shard_map/ppermute | solution.py:53
  24.2 10.2 %collective-permute-start.6 = (bf16[128,2048]{1,0:T(8,128)(2,1)S(1)}, bf16[128,2048]{1,0:T(8,128)(2,1)S(1)}, u32[]{:S(2)}, u32[]{:S(2)}) collective-permute-start(bf16[128,2048]{1,0:T(8,128)(2,1)S(1)} %pad_maximum_fusion.2), channel_id=1, source_target_pairs={{0,96},{32,64},{64,32},{96,0},{16,48},{48,16},{80,112},{112,80},{1... | collective-permute-start | bytes 1572872 | tf_op jit(solution)/shard_map/ppermute | solution.py:53
  29.7 14.9 %copy-start.1 = (bf16[1024,2048]{1,0:T(8,128)(2,1)S(1)}, bf16[1024,2048]{1,0:T(8,128)(2,1)}, u32[]{:S(2)}) copy-start(bf16[1024,2048]{1,0:T(8,128)(2,1)} %param.3) | copy-start | bytes 12582916
  29.8 10.5 %collective-permute-start.2 = (bf16[128,2048]{1,0:T(8,128)(2,1)S(1)}, bf16[128,2048]{1,0:T(8,128)(2,1)S(1)}, u32[]{:S(2)}, u32[]{:S(2)}) collective-permute-start(bf16[128,2048]{1,0:T(8,128)(2,1)S(1)} %pad_maximum_fusion.1), channel_id=1, source_target_pairs={{0,96},{32,64},{64,32},{96,0},{16,48},{48,16},{80,112},{112,80},{1... | collective-permute-start | bytes 1572872 | tf_op jit(solution)/shard_map/ppermute | solution.py:53
  34.5 13.0 %collective-permute-start.8 = (bf16[256,2048]{1,0:T(8,128)(2,1)S(1)}, bf16[256,2048]{1,0:T(8,128)(2,1)S(1)}, u32[]{:S(2)}, u32[]{:S(2)}) collective-permute-start(bf16[256,2048]{1,0:T(8,128)(2,1)S(1)} %constant_dynamic-update-slice_fusion), channel_id=1, source_target_pairs={{0,16},{16,0},{1,17},{17,1},{2,18},{18,2},{3,19},{19,3},{4,20},{20... | collective-permute-start | bytes 3145736 | tf_op jit(solution)/shard_map/ppermute | solution.py:76
  40.3 8.4 %collective-permute-start.7 = (bf16[256,2048]{1,0:T(8,128)(2,1)S(1)}, bf16[256,2048]{1,0:T(8,128)(2,1)S(1)}, u32[]{:S(2)}, u32[]{:S(2)}) collective-permute-start(bf16[256,2048]{1,0:T(8,128)(2,1)S(1)} %pad_maximum_fusion), channel_id=1, source_target_pairs={{0,16},{16,0},{1,17},{17,1},{2,18},{18,2},{3,19},{19,3},{4,20},{20... | collective-permute-start | bytes 3145736 | tf_op jit(solution)/shard_map/ppermute | solution.py:76
  50.5 10.2 %collective-permute-start.11 = (bf16[2,2,64,1024]{3,2,1,0:T(8,128)(2,1)S(1)}, bf16[2,2,64,1024]{3,2,1,0:T(8,128)(2,1)S(1)}, u32[]{:S(2)}, u32[]{:S(2)}) collective-permute-start(bf16[2,2,64,1024]{3,2,1,0:T(8,128)(2,1)S(1)} %pad_maximum_fusion.4), channel_id=1, source_target_pairs={{0,4},{4,0},{8,12},{12,8},{16,28},{20,24},{24,20},{28,16},{1,5},{5... | collective-permute-start | bytes 1572872 | tf_op jit(solution)/shard_map/ppermute | solution.py:53
  53.8 12.5 %collective-permute-start.9 = (bf16[2,2,64,1024]{3,2,1,0:T(8,128)(2,1)S(1)}, bf16[2,2,64,1024]{3,2,1,0:T(8,128)(2,1)S(1)}, u32[]{:S(2)}, u32[]{:S(2)}) collective-permute-start(bf16[2,2,64,1024]{3,2,1,0:T(8,128)(2,1)S(1)} %pad_maximum_fusion.3), channel_id=1, source_target_pairs={{0,4},{4,0},{8,12},{12,8},{16,28},{20,24},{24,20},{28,16},{1,5},{5... | collective-permute-start | bytes 1572872 | tf_op jit(solution)/shard_map/ppermute | solution.py:53
  60.9 10.5 %collective-permute-start.12 = (bf16[2,64,1024]{2,1,0:T(8,128)(2,1)S(1)}, bf16[2,64,1024]{2,1,0:T(8,128)(2,1)S(1)}, u32[]{:S(2)}, u32[]{:S(2)}) collective-permute-start(bf16[2,64,1024]{2,1,0:T(8,128)(2,1)S(1)} %fusion.1), channel_id=1, source_target_pairs={{0,12},{4,8},{8,4},{12,0},{16,20},{20,16},{24,28},{28,24},{1,13},{... | collective-permute-start | bytes 786440 | tf_op jit(solution)/shard_map/ppermute | solution.py:53
  66.5 19.4 %collective-permute-start.10 = (bf16[2,64,1024]{2,1,0:T(8,128)(2,1)S(1)}, bf16[2,64,1024]{2,1,0:T(8,128)(2,1)S(1)}, u32[]{:S(2)}, u32[]{:S(2)}) collective-permute-start(bf16[2,64,1024]{2,1,0:T(8,128)(2,1)S(1)} %fusion.6), channel_id=1, source_target_pairs={{0,12},{4,8},{8,4},{12,0},{16,20},{20,16},{24,28},{28,24},{1,13},{... | collective-permute-start | bytes 786440 | tf_op jit(solution)/shard_map/ppermute | solution.py:53
  71.5 18.8 %collective-permute-start.14 = (bf16[64,1024]{1,0:T(8,128)(2,1)S(1)}, bf16[64,1024]{1,0:T(8,128)(2,1)S(1)}, u32[]{:S(2)}, u32[]{:S(2)}) collective-permute-start(bf16[64,1024]{1,0:T(8,128)(2,1)S(1)} %get-tuple-element.38), channel_id=1, source_target_pairs={{0,1},{1,0},{2,3},{3,2},{16,19},{17,18},{18,17},{19,16},{4,5},{5,4... | collective-permute-start | bytes 393224 | tf_op jit(solution)/shard_map/ppermute | solution.py:53
  84.0 11.3 %collective-permute-start.13 = (bf16[64,1024]{1,0:T(8,128)(2,1)S(1)}, bf16[64,1024]{1,0:T(8,128)(2,1)S(1)}, u32[]{:S(2)}, u32[]{:S(2)}) collective-permute-start(bf16[64,1024]{1,0:T(8,128)(2,1)S(1)} %get-tuple-element.37), channel_id=1, source_target_pairs={{0,1},{1,0},{2,3},{3,2},{16,19},{17,18},{18,17},{19,16},{4,5},{5,4... | collective-permute-start | bytes 393224 | tf_op jit(solution)/shard_map/ppermute | solution.py:53
  90.3 13.8 %collective-permute-start.15 = (bf16[64,1024]{1,0:T(8,128)(2,1)S(1)}, bf16[64,1024]{1,0:T(8,128)(2,1)S(1)}, u32[]{:S(2)}, u32[]{:S(2)}) collective-permute-start(bf16[64,1024]{1,0:T(8,128)(2,1)S(1)} %fusion.10), channel_id=1, source_target_pairs={{0,3},{1,2},{2,1},{3,0},{16,17},{17,16},{18,19},{19,18},{4,7},{5,6... | collective-permute-start | bytes 393224 | tf_op jit(solution)/shard_map/ppermute | solution.py:53

commit v5 on v4

--- a/solution.py
+++ b/solution.py
@@ -24,6 +24,7 @@
         out_shape=jax.ShapeDtypeStruct(rows.shape, rows.dtype),
         in_specs=[pl.BlockSpec(memory_space=pltpu.VMEM)] * 2,
         out_specs=pl.BlockSpec(memory_space=pltpu.VMEM),
+        compiler_params=pltpu.CompilerParams(vmem_limit_bytes=8 * 1024 * 1024),
     )(rows, precond)
 
 
@@ -76,7 +77,7 @@
         both = [rows, lax.ppermute(rows, "core", [(0, 1), (1, 0)])]
         return [dot_t(r, train_grads).reshape(4, 2, count, width) for r in both]
 
-    parts = [partials(line[:2]), partials(line[2:])]
+    parts = [partials(line[0::2]), partials(line[1::2])]
 
     def block(home_x, home_zh):
         k = jnp.mod(zl - home_x, 4)
@@ -86,12 +87,12 @@
         m = [jnp.where(even_y, up, down), jnp.where(even_y, down, up)]
         found = [
             [
-                lax.dynamic_slice(part[c], (m[c], jnp.mod(k, 2), 0, 0), (1, 1, count, width))[0, 0]
+                lax.dynamic_slice(part[c], (m[c], k // 2, 0, 0), (1, 1, count, width))[0, 0]
                 for part in parts
             ]
             for c in range(2)
         ]
-        return jnp.concatenate([jnp.where(k < 2, *f) for f in found], axis=0)
+        return jnp.concatenate([jnp.where(jnp.mod(k, 2) == 0, *f) for f in found], axis=0)
 
     def sum_x(homes):
         def blocks(home_x):

time: 105 us -> 107 us (1.019)
  the two profiles are of different devices: /device:TPU:35 before, /device:TPU:8 now
where the time goes in v5:
time: 107 us
  starting transfers between devices  66.3 us (62%)
  waiting for transfers between devices  29.8 us (28%)
  matrix products  5.12 us (5%)
  other arithmetic  2.32 us (2%)
  local copies, waits for them, and re-layouts  2.04 us (2%)
    ppermute x11, starting transfers between devices, halve(): return lax.ppermute(array, names, pairs)  51.5 us
    ppermute x11, waiting for transfers between devices, halve(): return lax.ppermute(array, names, pairs)  28.5 us
    ppermute x3, starting transfers between devices, shift(): lax.ppermute(array, axis, [(i, (i + step) % size) for i in range(size)])  11 us
    dot_general x4, matrix products, dot_t(): lax.dot_general(rows, train, (((1,), (1,)), ((), ())), preferred_element_...  5.12 us
    ppermute x2, starting transfers between devices, partials(): both = [rows, lax.ppermute(rows, 'core', [(0, 1), (1, 0)])]  3.84 us
  transfers between devices with their start and end apart: 16, of which 10 were waited for; matrix products, arithmetic and copies ran while one was open for 5% of the time, Pallas kernels for 0%

profile of v5, /device:TPU:8, one launch (start us, length us, event | category | flops | bytes accessed | tf_op | source)
XLA Modules:
  0.0 106.8 jit_solution(16509676917812757423)
XLA Ops:
  0.0 0.0 copy-start
  0.0 1.0 copy-done
  1.0 0.0 copy-start.1
  1.0 0.9 copy-done.1
  1.9 0.2 shard_map.37
  2.2 3.8 %collective-permute-start.3 = (bf16[32,2048]{1,0:T(8,128)(2,1)S(1)}, bf16[32,2048]{1,0:T(8,128)(2,1)S(1)}, u32[]{:S(2)}, u32[]{:S(2)}) collective-permute-start(bf16[32,2048]{1,0:T(8,128)(2,1)S(1)} %shard_map.37), channel_id=1, source_target_pairs={{0,128},{128,256},{256,384},{384,0},{1,129},{129,257},{257,385},{3... | collective-permute-start | bytes 393224 | tf_op jit(solution)/shard_map/ppermute | solution.py:33
  6.0 4.6 %collective-permute-start.4 = (bf16[32,2048]{1,0:T(8,128)(2,1)S(1)}, bf16[32,2048]{1,0:T(8,128)(2,1)S(1)}, u32[]{:S(2)}, u32[]{:S(2)}) collective-permute-start(bf16[32,2048]{1,0:T(8,128)(2,1)S(1)} %shard_map.37), channel_id=1, source_target_pairs={{0,384},{128,0},{256,128},{384,256},{1,385},{129,1},{257,129},{385... | collective-permute-start | bytes 393224 | tf_op jit(solution)/shard_map/ppermute | solution.py:33
  10.7 2.6 %collective-permute-start = (bf16[32,2048]{1,0:T(8,128)(2,1)S(1)}, bf16[32,2048]{1,0:T(8,128)(2,1)S(1)}, u32[]{:S(2)}, u32[]{:S(2)}) collective-permute-start(bf16[32,2048]{1,0:T(8,128)(2,1)S(1)} %shard_map.37), channel_id=1, source_target_pairs={{0,256},{128,384},{256,0},{384,128},{1,257},{129,385},{257,1},{385... | collective-permute-start | bytes 393224 | tf_op jit(solution)/shard_map/ppermute | solution.py:33
  13.7 0.0 collective-permute-done.3
  13.7 1.3 %collective-permute-done.4 = bf16[32,2048]{1,0:T(8,128)(2,1)S(1)} collective-permute-done((bf16[32,2048]{1,0:T(8,128)(2,1)S(1)}, bf16[32,2048]{1,0:T(8,128)(2,1)S(1)}, u32[]{:S(2)}, u32[]{:S(2)}) %collective-permute-start.4) | collective-permute-done | bytes 131104 | tf_op jit(solution)/shard_map/ppermute | solution.py:33
  15.0 6.4 %collective-permute-start.5 = (bf16[64,2048]{1,0:T(8,128)(2,1)S(1)}, bf16[64,2048]{1,0:T(8,128)(2,1)S(1)}, u32[]{:S(2)}, u32[]{:S(2)}) collective-permute-start(bf16[64,2048]{1,0:T(8,128)(2,1)S(1)} %pad_maximum_fusion.6), channel_id=1, source_target_pairs={{0,32},{32,0},{64,96},{96,64},{16,112},{48,80},{80,48},{112,16},{1... | collective-permute-start | bytes 786440 | tf_op jit(solution)/shard_map/ppermute | solution.py:54
  21.5 0.0 collective-permute-done
  21.5 3.8 %collective-permute-start.1 = (bf16[64,2048]{1,0:T(8,128)(2,1)S(1)}, bf16[64,2048]{1,0:T(8,128)(2,1)S(1)}, u32[]{:S(2)}, u32[]{:S(2)}) collective-permute-start(bf16[64,2048]{1,0:T(8,128)(2,1)S(1)} %pad_maximum_fusion.5), channel_id=1, source_target_pairs={{0,32},{32,0},{64,96},{96,64},{16,112},{48,80},{80,48},{112,16},{1... | collective-permute-start | bytes 786440 | tf_op jit(solution)/shard_map/ppermute | solution.py:54
  25.4 0.4 collective-permute-done.5
  25.9 1.9 %collective-permute-start.6 = (bf16[128,2048]{1,0:T(8,128)(2,1)S(1)}, bf16[128,2048]{1,0:T(8,128)(2,1)S(1)}, u32[]{:S(2)}, u32[]{:S(2)}) collective-permute-start(bf16[128,2048]{1,0:T(8,128)(2,1)S(1)} %pad_maximum_fusion.2), channel_id=1, source_target_pairs={{0,96},{32,64},{64,32},{96,0},{16,48},{48,16},{80,112},{112,80},{1... | collective-permute-start | bytes 1572872 | tf_op jit(solution)/shard_map/ppermute | solution.py:54
  27.8 3.5 %collective-permute-done.1 = bf16[64,2048]{1,0:T(8,128)(2,1)S(1)} collective-permute-done((bf16[64,2048]{1,0:T(8,128)(2,1)S(1)}, bf16[64,2048]{1,0:T(8,128)(2,1)S(1)}, u32[]{:S(2)}, u32[]{:S(2)}) %collective-permute-start.1) | collective-permute-done | bytes 262176 | tf_op jit(solution)/shard_map/ppermute | solution.py:54
  31.3 0.0 copy-start.2
  31.3 3.0 %collective-permute-start.2 = (bf16[128,2048]{1,0:T(8,128)(2,1)S(1)}, bf16[128,2048]{1,0:T(8,128)(2,1)S(1)}, u32[]{:S(2)}, u32[]{:S(2)}) collective-permute-start(bf16[128,2048]{1,0:T(8,128)(2,1)S(1)} %pad_maximum_fusion.1), channel_id=1, source_target_pairs={{0,96},{32,64},{64,32},{96,0},{16,48},{48,16},{80,112},{112,80},{1... | collective-permute-start | bytes 1572872 | tf_op jit(solution)/shard_map/ppermute | solution.py:54
  34.4 2.6 %collective-permute-done.6 = bf16[128,2048]{1,0:T(8,128)(2,1)S(1)} collective-permute-done((bf16[128,2048]{1,0:T(8,128)(2,1)S(1)}, bf16[128,2048]{1,0:T(8,128)(2,1)S(1)}, u32[]{:S(2)}, u32[]{:S(2)}) %collective-permute-start.6) | collective-permute-done | bytes 524320 | tf_op jit(solution)/shard_map/ppermute | solution.py:54
  37.0 1.9 %collective-permute-start.8 = (bf16[256,2048]{1,0:T(8,128)(2,1)S(1)}, bf16[256,2048]{1,0:T(8,128)(2,1)S(1)}, u32[]{:S(2)}, u32[]{:S(2)}) collective-permute-start(bf16[256,2048]{1,0:T(8,128)(2,1)S(1)} %constant_dynamic-update-slice_fusion), channel_id=1, source_target_pairs={{0,16},{16,0},{1,17},{17,1},{2,18},{18,2},{3,19},{19,3},{4,20},{20... | collective-permute-start | bytes 3145736 | tf_op jit(solution)/shard_map/ppermute | solution.py:77
  38.9 3.7 %collective-permute-done.2 = bf16[128,2048]{1,0:T(8,128)(2,1)S(1)} collective-permute-done((bf16[128,2048]{1,0:T(8,128)(2,1)S(1)}, bf16[128,2048]{1,0:T(8,128)(2,1)S(1)}, u32[]{:S(2)}, u32[]{:S(2)}) %collective-permute-start.2) | collective-permute-done | bytes 524320 | tf_op jit(solution)/shard_map/ppermute | solution.py:54
  42.6 0.1 pad_maximum_fusion
  42.8 1.9 %collective-permute-start.7 = (bf16[256,2048]{1,0:T(8,128)(2,1)S(1)}, bf16[256,2048]{1,0:T(8,128)(2,1)S(1)}, u32[]{:S(2)}, u32[]{:S(2)}) collective-permute-start(bf16[256,2048]{1,0:T(8,128)(2,1)S(1)} %pad_maximum_fusion), channel_id=1, source_target_pairs={{0,16},{16,0},{1,17},{17,1},{2,18},{18,2},{3,19},{19,3},{4,20},{20... | collective-permute-start | bytes 3145736 | tf_op jit(solution)/shard_map/ppermute | solution.py:77
  44.7 0.0 copy-done.2
  44.7 1.3 %convolution_convert_fusion.2 = bf16[256,1024]{1,0:T(8,128)(2,1)S(1)} fusion(bf16[256,2048]{1,0:T(8,128)(2,1)S(1)} %constant_dynamic-update-slice_fusion, bf16[1024,2048]{1,0:T(8,128)(2,1)S(1)} %copy-done.2), kind=kOutput, calls=%fused_computation.2 | convolution fusion | flops 1074003968 | bytes 5767168 | tf_op jit(solution)/shard_map/dot_general | solution.py:37
  46.0 1.3 %convolution_convert_fusion.3 = bf16[256,1024]{1,0:T(8,128)(2,1)S(1)} fusion(bf16[1024,2048]{1,0:T(8,128)(2,1)S(1)} %copy-done.2, bf16[128,2048]{1,0:T(8,128)(2,1)S(1)} %collective-permute-done.2, bf16[64,2048]{1,0:T(8,128)(2,1)S(1)} %collective-permute-done.1, bf16[32,2048]{1,0:T(8,128)(2,1)S(1)} %collective-permute-done, bf16[32,2048]{1,0:T(8,128)(2,1)S(1)} %shard_map.37), kind=kOutput, calls=%fused_computation.3 | convolution fusion | flops 1078198272 | bytes 5767168 | tf_op jit(solution)/shard_map/dot_general | solution.py:37
  47.3 0.2 select_bitcast_fusion.15
  47.5 0.0 collective-permute-done.8
  47.5 1.3 %convolution_convert_fusion = bf16[256,1024]{1,0:T(8,128)(2,1)S(1)} fusion(bf16[256,2048]{1,0:T(8,128)(2,1)S(1)} %collective-permute-done.8, bf16[1024,2048]{1,0:T(8,128)(2,1)S(1)} %copy-done.2), kind=kOutput, calls=%fused_computation | convolution fusion | flops 1074003968 | bytes 5767168 | tf_op jit(solution)/shard_map/dot_general | solution.py:37
  48.8 0.0 collective-permute-done.7
  48.8 1.3 %convolution_convert_fusion.1 = bf16[256,1024]{1,0:T(8,128)(2,1)S(1)} fusion(bf16[256,2048]{1,0:T(8,128)(2,1)S(1)} %collective-permute-done.7, bf16[1024,2048]{1,0:T(8,128)(2,1)S(1)} %copy-done.2), kind=kOutput, calls=%fused_computation.1 | convolution fusion | flops 1074003968 | bytes 5767168 | tf_op jit(solution)/shard_map/dot_general | solution.py:37
  50.1 0.2 select_bitcast_fusion.14
  50.5 0.1 pad_maximum_fusion.4
  50.5 2.2 %collective-permute-start.11 = (bf16[2,2,64,1024]{3,2,1,0:T(8,128)(2,1)S(1)}, bf16[2,2,64,1024]{3,2,1,0:T(8,128)(2,1)S(1)}, u32[]{:S(2)}, u32[]{:S(2)}) collective-permute-start(bf16[2,2,64,1024]{3,2,1,0:T(8,128)(2,1)S(1)} %pad_maximum_fusion.4), channel_id=1, source_target_pairs={{0,4},{4,0},{8,12},{12,8},{16,28},{20,24},{24,20},{28,16},{1,5},{5... | collective-permute-start | bytes 1572872 | tf_op jit(solution)/shard_map/ppermute | solution.py:54
  52.9 0.1 pad_maximum_fusion.3
  53.0 3.6 %collective-permute-start.9 = (bf16[2,2,64,1024]{3,2,1,0:T(8,128)(2,1)S(1)}, bf16[2,2,64,1024]{3,2,1,0:T(8,128)(2,1)S(1)}, u32[]{:S(2)}, u32[]{:S(2)}) collective-permute-start(bf16[2,2,64,1024]{3,2,1,0:T(8,128)(2,1)S(1)} %pad_maximum_fusion.3), channel_id=1, source_target_pairs={{0,4},{4,0},{8,12},{12,8},{16,28},{20,24},{24,20},{28,16},{1,5},{5... | collective-permute-start | bytes 1572872 | tf_op jit(solution)/shard_map/ppermute | solution.py:54
  56.7 4.9 %collective-permute-done.11 = bf16[2,2,64,1024]{3,2,1,0:T(8,128)(2,1)S(1)} collective-permute-done((bf16[2,2,64,1024]{3,2,1,0:T(8,128)(2,1)S(1)}, bf16[2,2,64,1024]{3,2,1,0:T(8,128)(2,1)S(1)}, u32[]{:S(2)}, u32[]{:S(2)}) %collective-permute-start.11) | collective-permute-done | bytes 524320 | tf_op jit(solution)/shard_map/ppermute | solution.py:54
  61.6 0.1 convert_element_type.70
  61.7 0.1 fusion.1
  61.8 3.5 %collective-permute-start.12 = (bf16[2,64,1024]{2,1,0:T(8,128)(2,1)S(1)}, bf16[2,64,1024]{2,1,0:T(8,128)(2,1)S(1)}, u32[]{:S(2)}, u32[]{:S(2)}) collective-permute-start(bf16[2,64,1024]{2,1,0:T(8,128)(2,1)S(1)} %fusion.1), channel_id=1, source_target_pairs={{0,12},{4,8},{8,4},{12,0},{16,20},{20,16},{24,28},{28,24},{1,13},{... | collective-permute-start | bytes 786440 | tf_op jit(solution)/shard_map/ppermute | solution.py:54
  65.3 2.2 %collective-permute-done.9 = bf16[2,2,64,1024]{3,2,1,0:T(8,128)(2,1)S(1)} collective-permute-done((bf16[2,2,64,1024]{3,2,1,0:T(8,128)(2,1)S(1)}, bf16[2,2,64,1024]{3,2,1,0:T(8,128)(2,1)S(1)}, u32[]{:S(2)}, u32[]{:S(2)}) %collective-permute-start.9) | collective-permute-done | bytes 524320 | tf_op jit(solution)/shard_map/ppermute | solution.py:54
  67.6 0.1 convert_element_type.65
  67.7 0.1 fusion.6
  67.7 3.5 %collective-permute-start.10 = (bf16[2,64,1024]{2,1,0:T(8,128)(2,1)S(1)}, bf16[2,64,1024]{2,1,0:T(8,128)(2,1)S(1)}, u32[]{:S(2)}, u32[]{:S(2)}) collective-permute-start(bf16[2,64,1024]{2,1,0:T(8,128)(2,1)S(1)} %fusion.6), channel_id=1, source_target_pairs={{0,12},{4,8},{8,4},{12,0},{16,20},{20,16},{24,28},{28,24},{1,13},{... | collective-permute-start | bytes 786440 | tf_op jit(solution)/shard_map/ppermute | solution.py:54
  71.2 0.0 collective-permute-done.12
  71.3 0.1 fusion.4
  71.4 9.1 %collective-permute-start.14 = (bf16[64,1024]{1,0:T(8,128)(2,1)S(1)}, bf16[64,1024]{1,0:T(8,128)(2,1)S(1)}, u32[]{:S(2)}, u32[]{:S(2)}) collective-permute-start(bf16[64,1024]{1,0:T(8,128)(2,1)S(1)} %get-tuple-element.38), channel_id=1, source_target_pairs={{0,1},{1,0},{2,3},{3,2},{16,19},{17,18},{18,17},{19,16},{4,5},{5,4... | collective-permute-start | bytes 393224 | tf_op jit(solution)/shard_map/ppermute | solution.py:54
  80.5 1.9 %collective-permute-start.13 = (bf16[64,1024]{1,0:T(8,128)(2,1)S(1)}, bf16[64,1024]{1,0:T(8,128)(2,1)S(1)}, u32[]{:S(2)}, u32[]{:S(2)}) collective-permute-start(bf16[64,1024]{1,0:T(8,128)(2,1)S(1)} %get-tuple-element.37), channel_id=1, source_target_pairs={{0,1},{1,0},{2,3},{3,2},{16,19},{17,18},{18,17},{19,16},{4,5},{5,4... | collective-permute-start | bytes 393224 | tf_op jit(solution)/shard_map/ppermute | solution.py:54
  82.4 0.0 collective-permute-done.10
  82.4 0.1 fusion.8
  82.5 2.8 %collective-permute-done.14 = bf16[64,1024]{1,0:T(8,128)(2,1)S(1)} collective-permute-done((bf16[64,1024]{1,0:T(8,128)(2,1)S(1)}, bf16[64,1024]{1,0:T(8,128)(2,1)S(1)}, u32[]{:S(2)}, u32[]{:S(2)}) %collective-permute-start.14) | collective-permute-done | bytes 131104 | tf_op jit(solution)/shard_map/ppermute | solution.py:54
  85.4 12.4 %collective-permute-start.15 = (bf16[64,1024]{1,0:T(8,128)(2,1)S(1)}, bf16[64,1024]{1,0:T(8,128)(2,1)S(1)}, u32[]{:S(2)}, u32[]{:S(2)}) collective-permute-start(bf16[64,1024]{1,0:T(8,128)(2,1)S(1)} %fusion.10), channel_id=1, source_target_pairs={{0,3},{1,2},{2,1},{3,0},{16,17},{17,16},{18,19},{19,18},{4,7},{5,6... | collective-permute-start | bytes 393224 | tf_op jit(solution)/shard_map/ppermute | solution.py:54
  97.8 3.0 %collective-permute-done.13 = bf16[64,1024]{1,0:T(8,128)(2,1)S(1)} collective-permute-done((bf16[64,1024]{1,0:T(8,128)(2,1)S(1)}, bf16[64,1024]{1,0:T(8,128)(2,1)S(1)}, u32[]{:S(2)}, u32[]{:S(2)}) %collective-permute-start.13) | collective-permute-done | bytes 131104 | tf_op jit(solution)/shard_map/ppermute | solution.py:54
  100.8 5.3 %collective-permute-done.15 = bf16[64,1024]{1,0:T(8,128)(2,1)S(1)} collective-permute-done((bf16[64,1024]{1,0:T(8,128)(2,1)S(1)}, bf16[64,1024]{1,0:T(8,128)(2,1)S(1)}, u32[]{:S(2)}, u32[]{:S(2)}) %collective-permute-start.15) | collective-permute-done | bytes 131104 | tf_op jit(solution)/shard_map/ppermute | solution.py:54
  106.1 0.7 reverse_select_fusion
  (23 shorter events, 0.6 us)
Async XLA Ops:
  0.0 1.0 copy-start
  1.0 0.9 copy-start.1
  2.2 11.5 %collective-permute-start.3 = (bf16[32,2048]{1,0:T(8,128)(2,1)S(1)}, bf16[32,2048]{1,0:T(8,128)(2,1)S(1)}, u32[]{:S(2)}, u32[]{:S(2)}) collective-permute-start(bf16[32,2048]{1,0:T(8,128)(2,1)S(1)} %shard_map.37), channel_id=1, source_target_pairs={{0,128},{128,256},{256,384},{384,0},{1,129},{129,257},{257,385},{3... | collective-permute-start | bytes 393224 | tf_op jit(solution)/shard_map/ppermute | solution.py:33
  6.0 9.0 %collective-permute-start.4 = (bf16[32,2048]{1,0:T(8,128)(2,1)S(1)}, bf16[32,2048]{1,0:T(8,128)(2,1)S(1)}, u32[]{:S(2)}, u32[]{:S(2)}) collective-permute-start(bf16[32,2048]{1,0:T(8,128)(2,1)S(1)} %shard_map.37), channel_id=1, source_target_pairs={{0,384},{128,0},{256,128},{384,256},{1,385},{129,1},{257,129},{385... | collective-permute-start | bytes 393224 | tf_op jit(solution)/shard_map/ppermute | solution.py:33
  10.7 10.8 %collective-permute-start = (bf16[32,2048]{1,0:T(8,128)(2,1)S(1)}, bf16[32,2048]{1,0:T(8,128)(2,1)S(1)}, u32[]{:S(2)}, u32[]{:S(2)}) collective-permute-start(bf16[32,2048]{1,0:T(8,128)(2,1)S(1)} %shard_map.37), channel_id=1, source_target_pairs={{0,256},{128,384},{256,0},{384,128},{1,257},{129,385},{257,1},{385... | collective-permute-start | bytes 393224 | tf_op jit(solution)/shard_map/ppermute | solution.py:33
  15.0 10.8 %collective-permute-start.5 = (bf16[64,2048]{1,0:T(8,128)(2,1)S(1)}, bf16[64,2048]{1,0:T(8,128)(2,1)S(1)}, u32[]{:S(2)}, u32[]{:S(2)}) collective-permute-start(bf16[64,2048]{1,0:T(8,128)(2,1)S(1)} %pad_maximum_fusion.6), channel_id=1, source_target_pairs={{0,32},{32,0},{64,96},{96,64},{16,112},{48,80},{80,48},{112,16},{1... | collective-permute-start | bytes 786440 | tf_op jit(solution)/shard_map/ppermute | solution.py:54
  21.5 9.7 %collective-permute-start.1 = (bf16[64,2048]{1,0:T(8,128)(2,1)S(1)}, bf16[64,2048]{1,0:T(8,128)(2,1)S(1)}, u32[]{:S(2)}, u32[]{:S(2)}) collective-permute-start(bf16[64,2048]{1,0:T(8,128)(2,1)S(1)} %pad_maximum_fusion.5), channel_id=1, source_target_pairs={{0,32},{32,0},{64,96},{96,64},{16,112},{48,80},{80,48},{112,16},{1... | collective-permute-start | bytes 786440 | tf_op jit(solution)/shard_map/ppermute | solution.py:54
  25.9 11.1 %collective-permute-start.6 = (bf16[128,2048]{1,0:T(8,128)(2,1)S(1)}, bf16[128,2048]{1,0:T(8,128)(2,1)S(1)}, u32[]{:S(2)}, u32[]{:S(2)}) collective-permute-start(bf16[128,2048]{1,0:T(8,128)(2,1)S(1)} %pad_maximum_fusion.2), channel_id=1, source_target_pairs={{0,96},{32,64},{64,32},{96,0},{16,48},{48,16},{80,112},{112,80},{1... | collective-permute-start | bytes 1572872 | tf_op jit(solution)/shard_map/ppermute | solution.py:54
  31.3 13.4 %copy-start.2 = (bf16[1024,2048]{1,0:T(8,128)(2,1)S(1)}, bf16[1024,2048]{1,0:T(8,128)(2,1)}, u32[]{:S(2)}) copy-start(bf16[1024,2048]{1,0:T(8,128)(2,1)} %param.3) | copy-start | bytes 12582916
  31.3 11.3 %collective-permute-start.2 = (bf16[128,2048]{1,0:T(8,128)(2,1)S(1)}, bf16[128,2048]{1,0:T(8,128)(2,1)S(1)}, u32[]{:S(2)}, u32[]{:S(2)}) collective-permute-start(bf16[128,2048]{1,0:T(8,128)(2,1)S(1)} %pad_maximum_fusion.1), channel_id=1, source_target_pairs={{0,96},{32,64},{64,32},{96,0},{16,48},{48,16},{80,112},{112,80},{1... | collective-permute-start | bytes 1572872 | tf_op jit(solution)/shard_map/ppermute | solution.py:54
  37.0 10.5 %collective-permute-start.8 = (bf16[256,2048]{1,0:T(8,128)(2,1)S(1)}, bf16[256,2048]{1,0:T(8,128)(2,1)S(1)}, u32[]{:S(2)}, u32[]{:S(2)}) collective-permute-start(bf16[256,2048]{1,0:T(8,128)(2,1)S(1)} %constant_dynamic-update-slice_fusion), channel_id=1, source_target_pairs={{0,16},{16,0},{1,17},{17,1},{2,18},{18,2},{3,19},{19,3},{4,20},{20... | collective-permute-start | bytes 3145736 | tf_op jit(solution)/shard_map/ppermute | solution.py:77
  42.8 6.1 %collective-permute-start.7 = (bf16[256,2048]{1,0:T(8,128)(2,1)S(1)}, bf16[256,2048]{1,0:T(8,128)(2,1)S(1)}, u32[]{:S(2)}, u32[]{:S(2)}) collective-permute-start(bf16[256,2048]{1,0:T(8,128)(2,1)S(1)} %pad_maximum_fusion), channel_id=1, source_target_pairs={{0,16},{16,0},{1,17},{17,1},{2,18},{18,2},{3,19},{19,3},{4,20},{20... | collective-permute-start | bytes 3145736 | tf_op jit(solution)/shard_map/ppermute | solution.py:77
  50.5 11.1 %collective-permute-start.11 = (bf16[2,2,64,1024]{3,2,1,0:T(8,128)(2,1)S(1)}, bf16[2,2,64,1024]{3,2,1,0:T(8,128)(2,1)S(1)}, u32[]{:S(2)}, u32[]{:S(2)}) collective-permute-start(bf16[2,2,64,1024]{3,2,1,0:T(8,128)(2,1)S(1)} %pad_maximum_fusion.4), channel_id=1, source_target_pairs={{0,4},{4,0},{8,12},{12,8},{16,28},{20,24},{24,20},{28,16},{1,5},{5... | collective-permute-start | bytes 1572872 | tf_op jit(solution)/shard_map/ppermute | solution.py:54
  53.0 14.6 %collective-permute-start.9 = (bf16[2,2,64,1024]{3,2,1,0:T(8,128)(2,1)S(1)}, bf16[2,2,64,1024]{3,2,1,0:T(8,128)(2,1)S(1)}, u32[]{:S(2)}, u32[]{:S(2)}) collective-permute-start(bf16[2,2,64,1024]{3,2,1,0:T(8,128)(2,1)S(1)} %pad_maximum_fusion.3), channel_id=1, source_target_pairs={{0,4},{4,0},{8,12},{12,8},{16,28},{20,24},{24,20},{28,16},{1,5},{5... | collective-permute-start | bytes 1572872 | tf_op jit(solution)/shard_map/ppermute | solution.py:54
  61.8 9.5 %collective-permute-start.12 = (bf16[2,64,1024]{2,1,0:T(8,128)(2,1)S(1)}, bf16[2,64,1024]{2,1,0:T(8,128)(2,1)S(1)}, u32[]{:S(2)}, u32[]{:S(2)}) collective-permute-start(bf16[2,64,1024]{2,1,0:T(8,128)(2,1)S(1)} %fusion.1), channel_id=1, source_target_pairs={{0,12},{4,8},{8,4},{12,0},{16,20},{20,16},{24,28},{28,24},{1,13},{... | collective-permute-start | bytes 786440 | tf_op jit(solution)/shard_map/ppermute | solution.py:54
  67.7 14.7 %collective-permute-start.10 = (bf16[2,64,1024]{2,1,0:T(8,128)(2,1)S(1)}, bf16[2,64,1024]{2,1,0:T(8,128)(2,1)S(1)}, u32[]{:S(2)}, u32[]{:S(2)}) collective-permute-start(bf16[2,64,1024]{2,1,0:T(8,128)(2,1)S(1)} %fusion.6), channel_id=1, source_target_pairs={{0,12},{4,8},{8,4},{12,0},{16,20},{20,16},{24,28},{28,24},{1,13},{... | collective-permute-start | bytes 786440 | tf_op jit(solution)/shard_map/ppermute | solution.py:54
  71.4 14.0 %collective-permute-start.14 = (bf16[64,1024]{1,0:T(8,128)(2,1)S(1)}, bf16[64,1024]{1,0:T(8,128)(2,1)S(1)}, u32[]{:S(2)}, u32[]{:S(2)}) collective-permute-start(bf16[64,1024]{1,0:T(8,128)(2,1)S(1)} %get-tuple-element.38), channel_id=1, source_target_pairs={{0,1},{1,0},{2,3},{3,2},{16,19},{17,18},{18,17},{19,16},{4,5},{5,4... | collective-permute-start | bytes 393224 | tf_op jit(solution)/shard_map/ppermute | solution.py:54
  80.5 20.3 %collective-permute-start.13 = (bf16[64,1024]{1,0:T(8,128)(2,1)S(1)}, bf16[64,1024]{1,0:T(8,128)(2,1)S(1)}, u32[]{:S(2)}, u32[]{:S(2)}) collective-permute-start(bf16[64,1024]{1,0:T(8,128)(2,1)S(1)} %get-tuple-element.37), channel_id=1, source_target_pairs={{0,1},{1,0},{2,3},{3,2},{16,19},{17,18},{18,17},{19,16},{4,5},{5,4... | collective-permute-start | bytes 393224 | tf_op jit(solution)/shard_map/ppermute | solution.py:54
  85.4 20.7 %collective-permute-start.15 = (bf16[64,1024]{1,0:T(8,128)(2,1)S(1)}, bf16[64,1024]{1,0:T(8,128)(2,1)S(1)}, u32[]{:S(2)}, u32[]{:S(2)}) collective-permute-start(bf16[64,1024]{1,0:T(8,128)(2,1)S(1)} %fusion.10), channel_id=1, source_target_pairs={{0,3},{1,2},{2,1},{3,0},{16,17},{17,16},{18,19},{19,18},{4,7},{5,6... | collective-permute-start | bytes 393224 | tf_op jit(solution)/shard_map/ppermute | solution.py:54
